TPU v7x, 128 devices: a whole 4x4x4 slice. The times are simulated.
128 devices in a mesh: member: 4 (over y_lo, core), fsdp: 32 (over x, y_hi, z).
Axes of the slice: x: 4, y: 4 (y_hi: 2, y_lo: 2; y = y_hi * 2 + y_lo), z: 4, core: 2. Of those that a mesh axis runs over, the one named last changes fastest.
Arguments:
- tokens: bfloat16 [8, 512, 8192], P('member', 'fsdp'), may hold values from -6 to 6
- weights: bfloat16 [8, 8192, 16384], P('member', None, 'fsdp'), may hold values from -6 to 6
- targets: bfloat16 [8, 512, 16384], P('member', None, 'fsdp'), may hold values from -6 to 6
- live: int32 [8], P('member'), may hold values from 64 to 512, as said below
Outputs:
- merged: float32 [8192, 16384], P('member', 'fsdp')
Inputs may be any that keep to these rules, and one draw needn't show every extreme that they name: Every draw has some task with all 512 rows live.
All inputs are finite; a program needn't handle non-finite values.
Results may differ from a plain program's by a relative error of at most 0.0035.
Values may be sent and summed in bfloat16 or wider, within the bound.
A program may use at most 256 MiB of HBM per device.

v0:
```python
import jax
import jax.numpy as jnp
from jax import lax
from jax.sharding import PartitionSpec as P

D = 8192


def block_resid(rows, wanted, weight, count, scale):
    outputs = jnp.dot(rows, weight, preferred_element_type=jnp.float32) * scale
    row_ids = jnp.arange(rows.shape[0], dtype=jnp.int32)
    keep = (row_ids < count)[:, None]
    return jnp.where(keep, outputs - wanted.astype(jnp.float32), 0.0).astype(jnp.bfloat16)


def residual(gathered, weight, target, count, scale):
    return block_resid(gathered, target, weight, count, scale)


def contract_rows(inputs, resid, scale):
    return (
        lax.dot_general(inputs, resid, (((0,), (0,)), ((), ())), preferred_element_type=jnp.float32)
        * scale
    )


def shards(tokens, weights, targets, live):
    scale = D ** (-0.5)
    task_count = tokens.shape[0]
    gathered_all = []
    resids = []
    for task in range(task_count):
        gathered = lax.all_gather(tokens[task], "fsdp", axis=0, tiled=True)
        gathered_all.append(gathered)
        resids.append(residual(gathered, weights[task], targets[task], live[task], scale))
    grads = [contract_rows(gathered_all[task], resids[task], scale) for task in range(task_count)]
    numer = jnp.zeros(grads[0].shape, jnp.float32)
    denom = jnp.zeros(grads[0].shape, jnp.float32)
    for task in range(task_count):
        fisher = grads[task] * grads[task]
        numer = numer + fisher * weights[task].astype(jnp.float32)
        denom = denom + fisher
    numer_share, denom_share = (
        lax.psum_scatter(numer, "member", scatter_dimension=0, tiled=True),
        lax.psum_scatter(denom, "member", scatter_dimension=0, tiled=True),
    )
    return numer_share / jnp.maximum(denom_share, 0.02)


def solution(mesh):
    in_specs = (
        P("member", "fsdp", None),
        P("member", None, "fsdp"),
        P("member", None, "fsdp"),
        P("member"),
    )
    out_specs = P("member", "fsdp")
    return jax.shard_map(shards, mesh=mesh, in_specs=in_specs, out_specs=out_specs, check_vma=False)
```

profile of v0, /device:TPU:1, one launch (start us, length us, event | category | flops | bytes accessed | tf_op | source)
XLA Modules:
  0.0 573.2 jit_solution(6059038433557997347)
XLA Ops:
  6.5 0.0 all-gather.7.cloned.1.call-start
  6.5 1.9 fusion.54
  8.4 0.0 all-gather.7.cloned.1.call-update
  8.4 0.0 all-gather.5.cloned.1.call-start
  8.5 0.7 all-gather.5.cloned.1.call-update
  9.2 0.0 reduce-scatter.5.cloned.1.call-start
  9.2 11.3 %fusion.53 = (bf16[1,8192,512]{2,1,0:T(8,128)(2,1)}, bf16[1,8192,512]{2,1,0:T(8,128)(2,1)}) fusion(bf16[2,8192,512]{2,1,0:T(8,128)(2,1)} %param.5), kind=kLoop, calls=%fused_computation.29 | loop fusion | bytes 33554432 | tf_op jit(solution)/shard_map/slice | solution.py:35
  20.5 11.6 %copy.8 = bf16[1,8192,512]{1,2,0:T(8,128)(2,1)} copy(bf16[1,8192,512]{2,1,0:T(8,128)(2,1)} %get-tuple-element.7) | data formatting | bytes 16777216
  32.1 0.0 copy-start.1
  32.1 0.0 copy-start.2
  32.1 12.0 %copy.9 = bf16[1,8192,512]{1,2,0:T(8,128)(2,1)} copy(bf16[1,8192,512]{2,1,0:T(8,128)(2,1)} %get-tuple-element.8) | data formatting | bytes 16777216
  44.1 0.0 copy-done.1
  44.1 0.6 fusion.55
  44.8 0.6 iota_compare_fusion
  45.4 0.6 iota_compare_fusion.1
  46.0 71.7 %all-gather.7.cloned.1.call-done = bf16[1,512,8192]{2,1,0:T(8,128)(2,1)} async-done(((bf16[1,16,8192]{2,1,0:T(8,128)(2,1)}), bf16[1,512,8192]{2,1,0:T(8,128)(2,1)}) %all-gather.7.cloned.1.call-update) | async-done | bytes 8388624 | tf_op jit(solution)/shard_map/all_gather | solution.py:33
  117.6 0.0 copy-done.2
  117.6 0.0 copy-start
  117.6 10.4 %fusion.46 = bf16[512,512]{1,0:T(8,128)(2,1)S(1)} fusion(bf16[1,512,8192]{2,1,0:T(8,128)(2,1)} %all-gather.7.cloned.1.call-done, bf16[2,512,512]{2,1,0:T(8,128)(2,1)S(1)} %copy-done.2, pred[512]{0:T(512)(128)(4,1)S(1)} %iota_compare_fusion, bf16[2,8192,512]{2,1,0:T(8,128)(2,1)} %param.5), kind=kOutput, calls=%fused_computation.24 | convolution fusion | flops 4296278016 | bytes 17826304 | tf_op jit(solution)/shard_map/dot_general | solution.py:10
  128.0 0.0 copy-done
  128.1 8.2 %fusion.5 = f32[512,8192]{1,0:T(8,128)} fusion(bf16[512,512]{1,0:T(8,128)(2,1)S(1)} %fusion.46, bf16[1,512,8192]{2,1,0:T(8,128)(2,1)S(1)} %copy-done), kind=kOutput, calls=%fused_computation.10 | convolution fusion | flops 4294967296 | bytes 25690112 | tf_op jit(solution)/shard_map/dot_general | solution.py:22
  136.2 86.5 %all-gather.5.cloned.1.call-done = bf16[1,512,8192]{2,1,0:T(8,128)(2,1)} async-done(((bf16[1,16,8192]{2,1,0:T(8,128)(2,1)}), bf16[1,512,8192]{2,1,0:T(8,128)(2,1)}) %all-gather.5.cloned.1.call-update) | async-done | bytes 8388624 | tf_op jit(solution)/shard_map/all_gather | solution.py:33
  222.8 10.3 %fusion.41 = bf16[512,512]{1,0:T(8,128)(2,1)S(1)} fusion(bf16[1,512,8192]{2,1,0:T(8,128)(2,1)} %all-gather.5.cloned.1.call-done, bf16[2,512,512]{2,1,0:T(8,128)(2,1)S(1)} %copy-done.2, pred[512]{0:T(512)(128)(4,1)S(1)} %iota_compare_fusion.1, bf16[2,8192,512]{2,1,0:T(8,128)(2,1)} %param.5), kind=kOutput, calls=%fused_computation.23 | convolution fusion | flops 4296278016 | bytes 17826304 | tf_op jit(solution)/shard_map/dot_general | solution.py:10
  233.0 26.7 %bitcast_add_fusion = (f32[8192,512]{0,1:T(8,128)}, f32[8192,512]{0,1:T(8,128)}) fusion(f32[512,8192]{1,0:T(8,128)} %fusion.5, bf16[1,8192,512]{1,2,0:T(8,128)(2,1)} %copy.9, bf16[1,8192,512]{1,2,0:T(8,128)(2,1)} %copy.8, bf16[512,512]{1,0:T(8,128)(2,1)S(1)} %fusion.41, bf16[1,512,8192]{2,1,0:T(8,128)(2,1)} %all-gather.5.cloned.1.call-done), kind=kOutput, calls=%fused_computation | convolution fusion | flops 4336910336 | bytes 76021760 | tf_op jit(solution)/shard_map/dot_general | solution.py:22
  259.7 0.0 reduce-scatter.5.cloned.1.call-update
  259.7 0.0 reduce-scatter.3.cloned.1.call-start
  259.8 0.5 reduce-scatter.3.cloned.1.call-update
  260.3 144.4 %reduce-scatter.5.cloned.1.call-done = f32[2048,512]{0,1:T(8,128)} async-done(((f32[8192,512]{0,1:T(8,128)}), f32[2048,512]{0,1:T(8,128)}) %reduce-scatter.5.cloned.1.call-update) | async-done | bytes 4194320 | tf_op jit(solution)/shard_map/reduce_scatter | solution.py:45
  404.7 149.9 %reduce-scatter.3.cloned.1.call-done = f32[2048,512]{0,1:T(8,128)} async-done(((f32[8192,512]{0,1:T(8,128)}), f32[2048,512]{0,1:T(8,128)}) %reduce-scatter.3.cloned.1.call-update) | async-done | bytes 4194320 | tf_op jit(solution)/shard_map/reduce_scatter | solution.py:44
  554.6 6.7 %maximum_divide_fusion = f32[2048,512]{0,1:T(8,128)} fusion(f32[2048,512]{0,1:T(8,128)} %reduce-scatter.3.cloned.1.call-done, f32[2048,512]{0,1:T(8,128)} %reduce-scatter.5.cloned.1.call-done), kind=kLoop, calls=%fused_computation.16 | loop fusion | flops 2097152 | bytes 12582912 | tf_op jit(solution)/shard_map/div | solution.py:47
  561.3 5.3 copy.7
Async XLA Ops:
  6.5 111.1 %all-gather.7.cloned.1.call-start = ((), (), s32[]{:S(2)}) async-start(), calls=%async_computation.5 | async-start | bytes 8650752 | tf_op jit(solution)/shard_map/all_gather | solution.py:33
  8.4 214.3 %all-gather.5.cloned.1.call-start = ((), (), s32[]{:S(2)}) async-start(), calls=%async_computation.4 | async-start | bytes 8650752 | tf_op jit(solution)/shard_map/all_gather | solution.py:33
  9.2 395.5 %reduce-scatter.5.cloned.1.call-start = ((), (), s32[]{:S(2)}) async-start(), calls=%async_computation.3 | async-start | bytes 20971520 | tf_op jit(solution)/shard_map/reduce_scatter | solution.py:45
  32.1 12.0 %copy-start.1 = (s32[2]{0:T(128)S(1)}, s32[2]{0:T(128)}, u32[]{:S(2)}) copy-start(s32[2]{0:T(128)} %param.7) | copy-start | bytes 28
  32.1 85.5 %copy-start.2 = (bf16[2,512,512]{2,1,0:T(8,128)(2,1)S(1)}, bf16[2,512,512]{2,1,0:T(8,128)(2,1)}, u32[]{:S(2)}) copy-start(bf16[2,512,512]{2,1,0:T(8,128)(2,1)} %param.6) | copy-start | bytes 3145732
  117.6 10.4 %copy-start = (bf16[1,512,8192]{2,1,0:T(8,128)(2,1)S(1)}, bf16[1,512,8192]{2,1,0:T(8,128)(2,1)}, u32[]{:S(2)}) copy-start(bf16[1,512,8192]{2,1,0:T(8,128)(2,1)} %all-gather.7.cloned.1.call-done) | copy-start | bytes 25165828
  259.7 294.9 %reduce-scatter.3.cloned.1.call-start = ((), (), s32[]{:S(2)}) async-start(), calls=%async_computation.2 | async-start | bytes 20971520 | tf_op jit(solution)/shard_map/reduce_scatter | solution.py:44
Sparse Core Ops, SparseCore 0:
  10.5 107.0 all-gather.6
  120.7 101.9 all-gather.4
  259.8 144.8 reduce-scatter.4
  407.2 147.3 reduce-scatter.2
where the time goes:
time: 574 us; the launch traced here: 573 us
  waiting for transfers between devices  454 us (79%)
  matrix products  55.5 us (10%)
  local copies, waits for them, and re-layouts  42.7 us (7%)
  between operations  13.2 us (2%)
  other arithmetic  7.89 us (1%)
    all_gather x2, waiting for transfers between devices, shards(): gathered = lax.all_gather(tokens[task], 'fsdp', axis=0, tiled=True)  158 us
    reduce_scatter x1, waiting for transfers between devices, shards(): lax.psum_scatter(numer, 'member', scatter_dimension=0, tiled=True)  150 us
    reduce_scatter x1, waiting for transfers between devices, shards(): lax.psum_scatter(denom, 'member', scatter_dimension=0, tiled=True)  144 us
    dot_general x2, matrix products, contract_rows(): lax.dot_general(inputs, resid, (((0,), (0,)), ((), ())), preferred_elemen...  34.8 us
    unnamed x8, local copies, waits for them, and re-layouts  23.6 us
    dot_general x2, matrix products, block_resid(): outputs = jnp.dot(rows, weight, preferred_element_type=jnp.float32) * scale  20.7 us
  transfers between devices with their start and end apart: 4, of which 4 were waited for; matrix products, arithmetic and copies ran while one was open for 10% of the time, Pallas kernels for 0%

commit v1 on v0

v1 whole, which is shorter than its diff:
```python
import jax
import jax.numpy as jnp
from jax import lax
from jax.experimental import pallas as pl
from jax.experimental.pallas import tpu as pltpu
from jax.sharding import PartitionSpec as P

MESH = pl.DeviceIdType.MESH
D = 8192
SCALE = D ** (-0.5)
TOK = 512
COLS = 512
CHUNK = 1024
CHUNKS = D // CHUNK
ROWS = 256
QUARTER = D // 4
BLOCKS = QUARTER // ROWS
F32, BF16 = jnp.float32, jnp.bfloat16


def kernel(
    live, tok, wts, tgt, out,
    xg, wv, tv, acc, resid, s_nd, r_nd, y_nd, c_nd, stage,
    load_sem, g_send, g_recv, s_send, s_recv, y_send, y_recv, c_send, c_recv, out_sem,
):
    member = lax.axis_index("member")
    fsdp = lax.axis_index("fsdp")
    y_lo, core = member // 2, member % 2
    x, y_hi, z = fsdp // 8, (fsdp // 4) % 2, fsdp % 4
    xl, xr = (x + 3) % 4, (x + 1) % 4
    zl, zr = (z + 3) % 4, (z + 1) % 4
    to_xr, to_xl = (member, xr * 8 + y_hi * 4 + z), (member, xl * 8 + y_hi * 4 + z)
    to_zr, to_zl = (member, x * 8 + y_hi * 4 + zr), (member, x * 8 + y_hi * 4 + zl)
    to_hi = (member, x * 8 + (1 - y_hi) * 4 + z)
    to_core = (y_lo * 2 + 1 - core, fsdp)
    to_y = ((1 - y_lo) * 2 + core, fsdp)

    own = [
        pltpu.make_async_copy(
            tok.at[:, :, pl.ds(k * CHUNK, CHUNK)], xg.at[k, :, x, y_hi, z], load_sem.at[k]
        )
        for k in range(CHUNKS)
    ]
    for copy in own:
        copy.start()
    load_w = pltpu.make_async_copy(wts, wv, load_sem.at[CHUNKS])
    load_t = pltpu.make_async_copy(tgt, tv, load_sem.at[CHUNKS + 1])
    load_w.start()
    load_t.start()

    barrier = pltpu.get_barrier_semaphore()
    for peer in (to_xr, to_xl, to_zr, to_zl, to_hi, to_core, to_y):
        pl.semaphore_signal(barrier, inc=1, device_id=peer, device_id_type=MESH)
    pl.semaphore_wait(barrier, 7)

    def remote(src, dst, send, recv, peer):
        return pltpu.make_async_remote_copy(
            src_ref=src, dst_ref=dst, send_sem=send, recv_sem=recv, device_id=peer, device_id_type=MESH
        )

    def hops(step, k):
        if step == 0:
            return [(xg.at[k, :, x, y_hi, z], to_hi, xg.at[k, :, x, 1 - y_hi, z])]
        if step == 1:
            mine = [xg.at[k, t, x, :, z] for t in range(2)]
            return [
                (mine[0], to_xr, xg.at[k, 0, xl, :, z]),
                (mine[0], to_xl, xg.at[k, 0, xr, :, z]),
                (mine[1], to_zr, xg.at[k, 1, x, :, zl]),
                (mine[1], to_zl, xg.at[k, 1, x, :, zr]),
            ]
        x2, z2 = (x + 2) % 4, (z + 2) % 4
        if step == 2:
            return [
                (xg.at[k, 0, xl, 0, z], to_xr, xg.at[k, 0, x2, 0, z]),
                (xg.at[k, 0, xr, 1, z], to_xl, xg.at[k, 0, x2, 1, z]),
                (xg.at[k, 1, x, 0, zl], to_zr, xg.at[k, 1, x, 0, z2]),
                (xg.at[k, 1, x, 1, zr], to_zl, xg.at[k, 1, x, 1, z2]),
            ]
        if step == 3:
            return [
                (xg.at[k, 0, :, :, z], to_zr, xg.at[k, 0, :, :, zl]),
                (xg.at[k, 0, :, :, z], to_zl, xg.at[k, 0, :, :, zr]),
                (xg.at[k, 1, x], to_xr, xg.at[k, 1, xl]),
                (xg.at[k, 1, x], to_xl, xg.at[k, 1, xr]),
            ]
        return [
            (xg.at[k, 0, :, 0, zl], to_zr, xg.at[k, 0, :, 0, z2]),
            (xg.at[k, 0, :, 1, zr], to_zl, xg.at[k, 0, :, 1, z2]),
            (xg.at[k, 1, xl, 0], to_xr, xg.at[k, 1, x2, 0]),
            (xg.at[k, 1, xr, 1], to_xl, xg.at[k, 1, x2, 1]),
        ]

    def start(step, k):
        for i, (src, peer, _) in enumerate(hops(step, k)):
            remote(src, src, g_send.at[step, k, i], g_recv.at[step, k, i], peer).start()

    def landed(step, k):
        for i, (_, peer, dst) in enumerate(hops(step, k)):
            remote(dst, dst, g_send.at[step, k, i], g_recv.at[step, k, i], peer).wait_recv()

    def sent(step, k):
        for i, (src, peer, _) in enumerate(hops(step, k)):
            remote(src, src, g_send.at[step, k, i], g_recv.at[step, k, i], peer).wait_send()

    for k in range(CHUNKS):
        own[k].wait()
        start(0, k)
    acc[...] = jnp.zeros_like(acc)
    load_w.wait()

    def tick(i, carry):
        for step in (4, 3, 2, 1):
            k = i - step + 1

            @pl.when((k >= 0) & (k < CHUNKS))
            def _():
                landed(step - 1, k)
                start(step, k)

        k = i - 4

        @pl.when(k >= 0)
        def _():
            landed(4, k)
            for t in range(2):
                for half in range(2):
                    part = xg[k, t, pl.ds(half * 2, 2)].reshape(TOK // 2, CHUNK)
                    rows = pl.ds(pl.multiple_of(k * CHUNK, CHUNK), CHUNK)
                    acc[t, pl.ds(half * 256, 256), :] += jnp.dot(
                        part, wv[t, rows, :], preferred_element_type=F32
                    )

        return carry

    lax.fori_loop(0, CHUNKS + 4, tick, 0)

    load_t.wait()
    row_ids = lax.broadcasted_iota(jnp.int32, (TOK, COLS), 0)
    for t in range(2):
        diff = acc[t] * SCALE - tv[t].astype(F32)
        resid[t] = jnp.where(row_ids < live[t], diff, 0.0).astype(BF16)

    def sums(quarter, j):
        block = quarter * BLOCKS + j
        per = CHUNK // ROWS
        k, sub = block // per, block % per
        columns = pl.ds(pl.multiple_of(sub * ROWS, ROWS), ROWS)
        rows = pl.ds(pl.multiple_of(block * ROWS, ROWS), ROWS)
        numer = denom = None
        for t in range(2):
            inputs = xg[k, t, :, :, :, :, columns].reshape(TOK, ROWS)
            grad = SCALE * lax.dot_general(
                inputs, resid[t], (((0,), (0,)), ((), ())), preferred_element_type=F32
            )
            fisher = grad * grad
            term = fisher * wv[t, rows, :].astype(F32)
            numer = term if t == 0 else numer + term
            denom = fisher if t == 0 else denom + fisher
        return numer, denom

    far = (1 - y_lo) * 2
    near = y_lo * 2

    def to_sibling(j):
        return remote(s_nd.at[j], r_nd.at[j], s_send.at[j], s_recv.at[j], to_core)

    def to_partner(j):
        return remote(r_nd.at[j], y_nd.at[j], y_send.at[j], y_recv.at[j], to_y)

    def to_sibling_near(j):
        return remote(s_nd.at[j], c_nd.at[j], c_send.at[j], c_recv.at[j], to_core)

    def outward(i, carry):
        @pl.when(i < BLOCKS)
        def _():
            numer, denom = sums(far + 1 - core, i)
            s_nd[i, 0] = numer.astype(BF16)
            s_nd[i, 1] = denom.astype(BF16)
            to_sibling(i).start()

        @pl.when(i >= 1)
        def _():
            j = i - 1
            numer, denom = sums(far + core, j)
            to_sibling(j).wait_recv()
            r_nd[j, 0] = (numer + r_nd[j, 0].astype(F32)).astype(BF16)
            r_nd[j, 1] = (denom + r_nd[j, 1].astype(F32)).astype(BF16)
            to_partner(j).start()

        return carry

    lax.fori_loop(0, BLOCKS + 1, outward, 0)

    def write(j):
        rows = pl.ds(pl.multiple_of(j * ROWS, ROWS), ROWS)
        return pltpu.make_async_copy(stage.at[j % 2], out.at[rows], out_sem.at[j % 2])

    def inward(i, carry):
        @pl.when(i < BLOCKS)
        def _():
            numer, denom = sums(near + 1 - core, i)
            to_sibling(i).wait_send()
            s_nd[i, 0] = numer.astype(BF16)
            s_nd[i, 1] = denom.astype(BF16)
            to_sibling_near(i).start()

        @pl.when(i >= 1)
        def _():
            j = i - 1
            numer, denom = sums(near + core, j)
            to_sibling_near(j).wait_recv()
            numer = numer + c_nd[j, 0].astype(F32)
            denom = denom + c_nd[j, 1].astype(F32)
            to_partner(j).wait_recv()
            numer = numer + y_nd[j, 0].astype(F32)
            denom = denom + y_nd[j, 1].astype(F32)

            @pl.when(j >= 2)
            def _():
                write(j - 2).wait()

            stage[j % 2] = numer / jnp.maximum(denom, 0.02)
            write(j).start()

        return carry

    lax.fori_loop(0, BLOCKS + 1, inward, 0)

    def finish(j, carry):
        to_partner(j).wait_send()
        to_sibling_near(j).wait_send()
        return carry

    lax.fori_loop(0, BLOCKS, finish, 0)

    def finish_gather(k, carry):
        for step in range(5):
            sent(step, k)
        return carry

    lax.fori_loop(0, CHUNKS, finish_gather, 0)
    write(BLOCKS - 2).wait()
    write(BLOCKS - 1).wait()


def shards(tokens, weights, targets, live):
    dma = pltpu.SemaphoreType.DMA
    any_space = pl.BlockSpec(memory_space=pl.ANY)
    return pl.pallas_call(
        kernel,
        out_shape=jax.ShapeDtypeStruct((QUARTER, COLS), F32),
        in_specs=[pl.BlockSpec(memory_space=pltpu.SMEM), any_space, any_space, any_space],
        out_specs=any_space,
        scratch_shapes=[
            pltpu.VMEM((CHUNKS, 2, 4, 2, 4, 16, CHUNK), BF16),
            pltpu.VMEM((2, D, COLS), BF16),
            pltpu.VMEM((2, TOK, COLS), BF16),
            pltpu.VMEM((2, TOK, COLS), F32),
            pltpu.VMEM((2, TOK, COLS), BF16),
            pltpu.VMEM((BLOCKS, 2, ROWS, COLS), BF16),
            pltpu.VMEM((BLOCKS, 2, ROWS, COLS), BF16),
            pltpu.VMEM((BLOCKS, 2, ROWS, COLS), BF16),
            pltpu.VMEM((BLOCKS, 2, ROWS, COLS), BF16),
            pltpu.VMEM((2, ROWS, COLS), F32),
            dma((CHUNKS + 2,)),
            dma((5, CHUNKS, 4)),
            dma((5, CHUNKS, 4)),
            dma((BLOCKS,)),
            dma((BLOCKS,)),
            dma((BLOCKS,)),
            dma((BLOCKS,)),
            dma((BLOCKS,)),
            dma((BLOCKS,)),
            dma((2,)),
        ],
        compiler_params=pltpu.CompilerParams(
            collective_id=0, has_side_effects=True, vmem_limit_bytes=60 << 20
        ),
        cost_estimate=pl.CostEstimate(
            flops=2 * 2 * 2 * TOK * D * COLS, bytes_accessed=22 << 20, transcendentals=0
        ),
        name="merge",
    )(live, tokens, weights, targets)


def solution(mesh):
    in_specs = (
        P("member", "fsdp", None),
        P("member", None, "fsdp"),
        P("member", None, "fsdp"),
        P("member"),
    )
    out_specs = P("member", "fsdp")
    return jax.shard_map(shards, mesh=mesh, in_specs=in_specs, out_specs=out_specs, check_vma=False)
```

time: 574 us -> 210 us (0.37)
  waiting for transfers between devices: 454 us -> 0 us
  Pallas kernels: 0 us -> 205 us
  matrix products: 55.5 us -> 0 us
  local copies, waits for them, and re-layouts: 42.7 us -> 4.64 us
  between operations: 13.2 us -> 0.01 us
  other arithmetic: 7.89 us -> 0 us
    reduce_scatter x2 -> x0, waiting for transfers between devices: 294 us -> none  [the longest x1 150 us: shards(): lax.psum_scatter(numer, 'member', scatter_dimension=0, tiled=True)]
    pallas_call x0 -> x1, Pallas kernels: none -> 205 us  [shards(): pl.pallas_call(kernel, out_shape=jax.ShapeDtypeStruct((QUARTER, COLS), F3...]
    all_gather x2 -> x0, waiting for transfers between devices: 158 us -> none  [shards(): gathered = lax.all_gather(tokens[task], 'fsdp', axis=0, tiled=True)]
    dot_general x4 -> x0, matrix products: 55.5 us -> none  [the longest x2 34.8 us: contract_rows(): lax.dot_general(inputs, resid, (((0,), (0,)), ((), ())), preferred_elemen...]
    unnamed x8 -> x1, local copies, waits for them, and re-layouts: 23.6 us -> 4.64 us
    slice x3 -> x0, local copies, waits for them, and re-layouts: 13.8 us -> none  [the longest x1 11.3 us: shards(): weights[task]]
    div x1 -> x0, other arithmetic: 6.7 us -> none  [shards(): return numer_share / jnp.maximum(denom_share, 0.02)]
  transfers between devices with their start and end apart: 4 -> 0, of which waited for: 4 -> 0; matrix products, arithmetic and copies ran while one was open for 10% -> 0% of each run, Pallas kernels for 0% -> 0%
where the time goes in v1:
time: 210 us
  Pallas kernels  205 us (98%)
  local copies, waits for them, and re-layouts  4.64 us (2%)
    pallas_call x1, Pallas kernels, shards(): pl.pallas_call(kernel, out_shape=jax.ShapeDtypeStruct((QUARTER, COLS), F3...  205 us
    unnamed x1, local copies, waits for them, and re-layouts  4.64 us

profile of v1, /device:TPU:1, one launch (start us, length us, event | category | flops | bytes accessed | tf_op | source)
XLA Modules:
  0.0 209.7 jit_solution(6323121832280326777)
XLA Ops:
  0.0 205.1 %merge.1 = f32[2048,512]{1,0:T(8,128)} custom-call(s32[2]{0:T(128)} %live.1, bf16[2,16,8192]{2,1,0:T(8,128)(2,1)} %tok.1, bf16[2,8192,512]{2,1,0:T(8,128)(2,1)} %wts.1, bf16[2,512,512]{2,1,0:T(8,128)(2,1)} %tgt.1), custom_call_target="tpu_custom_call" | custom-call | flops 17179869184 | bytes 23068672 | tf_op jit(solution)/shard_map/merge/pallas_call | solution.py:250
  205.1 4.6 %copy.6 = f32[2048,512]{1,0:T(8,128)} copy(f32[2048,512]{1,0:T(8,128)} %merge.1) | data formatting | bytes 8388608

commit v2 on v1

v2 whole, which is shorter than its diff:
```python
import jax
import jax.numpy as jnp
from jax import lax
from jax.experimental import pallas as pl
from jax.experimental.pallas import tpu as pltpu
from jax.sharding import PartitionSpec as P

MESH = pl.DeviceIdType.MESH
D = 8192
SCALE = D ** (-0.5)
TOK = 512
COLS = 512
CHUNK = 1024
CHUNKS = D // CHUNK
EXTRA = CHUNKS // 2
ALL = CHUNKS + EXTRA
ROWS = 256
QUARTER = D // 4
BLOCKS = QUARTER // ROWS
SWAPPED = 3
SENT = BLOCKS - SWAPPED
F32, BF16 = jnp.float32, jnp.bfloat16


def kernel(
    live, tok, wts, tgt, out,
    xg, wv, wp, acc, resid, resid_p, r_n, y_n, c_s, c_r,
    load_sem, g_send, g_recv, w_send, w_recv, p_send, p_recv, s_send, s_recv, y_send, y_recv,
    c_send, c_recv, out_sem,
):
    member = lax.axis_index("member")
    fsdp = lax.axis_index("fsdp")
    y_lo, core = member // 2, member % 2
    x, y_hi, z = fsdp // 8, (fsdp // 4) % 2, fsdp % 4
    xl, xr = (x + 3) % 4, (x + 1) % 4
    zl, zr = (z + 3) % 4, (z + 1) % 4
    x2, z2 = (x + 2) % 4, (z + 2) % 4
    to_xr, to_xl = (member, xr * 8 + y_hi * 4 + z), (member, xl * 8 + y_hi * 4 + z)
    to_zr, to_zl = (member, x * 8 + y_hi * 4 + zr), (member, x * 8 + y_hi * 4 + zl)
    to_hi = (member, x * 8 + (1 - y_hi) * 4 + z)
    to_core = (y_lo * 2 + 1 - core, fsdp)
    to_y = ((1 - y_lo) * 2 + core, fsdp)
    to_alt = ((1 - y_lo) * 2 + core, x * 8 + (1 - y_hi) * 4 + z)

    own = [
        pltpu.make_async_copy(
            tok.at[:, :, pl.ds(k * CHUNK, CHUNK)], xg.at[k, :, x, y_hi, z], load_sem.at[k]
        )
        for k in range(CHUNKS)
    ]
    for copy in own:
        copy.start()
    load_w = pltpu.make_async_copy(wts, wv, load_sem.at[CHUNKS])
    load_w.start()
    load_t = [
        pltpu.make_async_copy(
            tgt.at[:, pl.ds(half * ROWS, ROWS)], c_s.at[pl.ds(0, 2), half], load_sem.at[CHUNKS + 1 + half]
        )
        for half in range(2)
    ]
    for copy in load_t:
        copy.start()

    barrier = pltpu.get_barrier_semaphore()
    for peer in (to_xr, to_xl, to_zr, to_zl, to_hi, to_core, to_y, to_alt):
        pl.semaphore_signal(barrier, inc=1, device_id=peer, device_id_type=MESH)
    pl.semaphore_wait(barrier, 8)

    def remote(src, dst, send, recv, peer):
        return pltpu.make_async_remote_copy(
            src_ref=src, dst_ref=dst, send_sem=send, recv_sem=recv, device_id=peer, device_id_type=MESH
        )

    def swap(k, hi):
        part = xg.at[k, :, x, hi, z]
        return remote(part, part, g_send.at[0, k, 0], g_recv.at[0, k, 0], to_hi)

    def extra(k, i):
        e, quarter = 2 * (k % 2) + i, (k // 2) % 2
        src = xg.at[k, :, x, :, z, :, pl.ds(i * 512, 512)]
        lanes = pl.ds(pl.multiple_of(quarter * 512, 512), 512)
        dst = xg.at[CHUNKS + e, :, x, :, z, :, lanes]
        sems = g_send.at[0, CHUNKS + e, quarter], g_recv.at[0, CHUNKS + e, quarter]
        return remote(src, dst, *sems, to_alt)

    def extra_in(k, quarter):
        dst = xg.at[k, :, x, :, z, :, pl.ds(quarter * 512, 512)]
        return remote(dst, dst, g_send.at[0, k, quarter], g_recv.at[0, k, quarter], to_alt)

    def hops(step, k):
        if step == 1:
            mine = [xg.at[k, t, x, :, z] for t in range(2)]
            return [
                (mine[0], to_xr, xg.at[k, 0, xl, :, z]),
                (mine[0], to_xl, xg.at[k, 0, xr, :, z]),
                (mine[1], to_zr, xg.at[k, 1, x, :, zl]),
                (mine[1], to_zl, xg.at[k, 1, x, :, zr]),
            ]
        if step == 2:
            return [
                (xg.at[k, 0, xl, 0, z], to_xr, xg.at[k, 0, x2, 0, z]),
                (xg.at[k, 0, xr, 1, z], to_xl, xg.at[k, 0, x2, 1, z]),
                (xg.at[k, 1, x, 0, zl], to_zr, xg.at[k, 1, x, 0, z2]),
                (xg.at[k, 1, x, 1, zr], to_zl, xg.at[k, 1, x, 1, z2]),
            ]
        if step == 3:
            return [
                (xg.at[k, 0, :, :, z], to_zr, xg.at[k, 0, :, :, zl]),
                (xg.at[k, 0, :, :, z], to_zl, xg.at[k, 0, :, :, zr]),
                (xg.at[k, 1, x], to_xr, xg.at[k, 1, xl]),
                (xg.at[k, 1, x], to_xl, xg.at[k, 1, xr]),
            ]
        return [
            (xg.at[k, 0, :, 0, zl], to_zr, xg.at[k, 0, :, 0, z2]),
            (xg.at[k, 0, :, 1, zr], to_zl, xg.at[k, 0, :, 1, z2]),
            (xg.at[k, 1, xl, 0], to_xr, xg.at[k, 1, x2, 0]),
            (xg.at[k, 1, xr, 1], to_xl, xg.at[k, 1, x2, 1]),
        ]

    def start(step, k):
        for i, (src, peer, _) in enumerate(hops(step, k)):
            remote(src, src, g_send.at[step, k, i], g_recv.at[step, k, i], peer).start()

    def landed(step, k):
        for i, (_, peer, dst) in enumerate(hops(step, k)):
            remote(dst, dst, g_send.at[step, k, i], g_recv.at[step, k, i], peer).wait_recv()

    def sent(step, k):
        for i, (src, peer, _) in enumerate(hops(step, k)):
            remote(src, src, g_send.at[step, k, i], g_recv.at[step, k, i], peer).wait_send()

    def weights_over(n):
        quarter, j = n % 2, n // 2
        rows = pl.ds(pl.multiple_of((1 - y_lo) * (D // 2) + quarter * QUARTER + j * ROWS, ROWS), ROWS)
        return remote(wts.at[:, rows], wp.at[n], w_send.at[n], w_recv.at[n], to_y)

    for k in range(CHUNKS):
        own[k].wait()
        swap(k, y_hi).start()
    acc[...] = jnp.zeros_like(acc)
    load_w.wait()

    def forward(i):
        for step in (4, 3, 2):
            k = i - step + 1

            @pl.when((k >= 0) & (k < ALL))
            def _():
                landed(step - 1, k)
                start(step, k)

    def tick(i, carry):
        forward(i)

        @pl.when(i < CHUNKS)
        def _():
            swap(i, 1 - y_hi).wait_recv()

        @pl.when(i >= CHUNKS)
        def _():
            for quarter in range(2):
                extra_in(i, quarter).wait_recv()

        start(1, i)

        @pl.when((i < CHUNKS) & (i // EXTRA == 1 - y_lo))
        def _():
            for piece in range(2):
                extra(i, piece).start()

        @pl.when((i >= 1) & (i <= 2 * SWAPPED))
        def _():
            weights_over(i - 1).start()

        k = i - 4

        @pl.when(k >= 0)
        def _():
            landed(4, k)
            rows = pl.ds(pl.multiple_of(k * CHUNK, CHUNK), CHUNK)
            for t in range(2):
                for half in range(2):
                    part = xg[k, t, pl.ds(half * 2, 2)].reshape(TOK // 2, CHUNK)
                    acc[t, pl.ds(half * 256, 256), :] += jnp.dot(
                        part, wv[t, rows, :], preferred_element_type=F32
                    )

        return carry

    lax.fori_loop(0, ALL, tick, 0)

    row_ids = lax.broadcasted_iota(jnp.int32, (TOK, COLS), 0)
    for copy in load_t:
        copy.wait()
    for t in range(2):
        diff = acc[t] * SCALE - c_s[t].reshape(TOK, COLS).astype(F32)
        resid[t] = jnp.where(row_ids < live[t], diff, 0.0).astype(BF16)
    resid_over = remote(resid, resid_p, p_send.at[0], p_recv.at[0], to_y)
    resid_over.start()

    def fisher_of(inputs, res):
        grad = SCALE * lax.dot_general(
            inputs.reshape(TOK, ROWS), res, (((0,), (0,)), ((), ())), preferred_element_type=F32
        )
        return grad * grad

    def own_sums(quarter, j, with_denom=True):
        block = quarter * BLOCKS + j
        per = CHUNK // ROWS
        columns = pl.ds(pl.multiple_of((block % per) * ROWS, ROWS), ROWS)
        rows = pl.ds(pl.multiple_of(block * ROWS, ROWS), ROWS)
        numer = denom = None
        for t in range(2):
            fisher = fisher_of(xg[block // per, t, :, :, :, :, columns], resid[t])
            term = fisher * wv[t, rows, :].astype(F32)
            numer = term if t == 0 else numer + term
            if with_denom:
                denom = fisher if t == 0 else denom + fisher
        return numer, denom

    far = (1 - y_lo) * 2
    near = y_lo * 2

    def to_sibling(i):
        return remote(c_s.at[i // 2, i % 2], r_n.at[i], s_send.at[i], s_recv.at[i], to_core)

    def to_partner(i):
        return remote(r_n.at[i], y_n.at[i], y_send.at[i], y_recv.at[i], to_y)

    def outward(i, carry):
        @pl.when(i < SENT)
        def _():
            c_s[i // 2, i % 2] = own_sums(far + 1 - core, SWAPPED + i, False)[0].astype(BF16)
            to_sibling(i).start()

        @pl.when(i >= 1)
        def _():
            n = i - 1
            numer, _ = own_sums(far + core, SWAPPED + n, False)
            to_sibling(n).wait_recv()
            r_n[n] = (numer + r_n[n].astype(F32)).astype(BF16)
            to_partner(n).start()

        return carry

    lax.fori_loop(0, SENT + 1, outward, 0)

    def both_sums(quarter, j, swapped):
        numer, denom = own_sums(near + quarter, j)
        columns = pl.ds(pl.multiple_of(quarter * 512 + (j % 2) * ROWS, ROWS), ROWS)
        for t in range(2):
            fisher = fisher_of(xg[CHUNKS + j // 2, t, :, :, :, :, columns], resid_p[t])
            if swapped:
                numer = numer + fisher * wp[2 * j + quarter, t].astype(F32)
            denom = denom + fisher
        return numer, denom

    def to_sibling_near(j):
        return remote(c_s.at[j % 4], c_r.at[j], c_send.at[j], c_recv.at[j], to_core)

    def left_sibling(i, carry):
        to_sibling(i).wait_send()
        return carry

    def pass_on(j, swapped):
        numer, denom = both_sums(1 - core, j, swapped)

        @pl.when(j >= 4)
        def _():
            to_sibling_near(j - 4).wait_send()

        @pl.when(j == 0)
        def _():
            lax.fori_loop(0, SENT, left_sibling, 0)

        c_s[j % 4, 0] = numer.astype(BF16)
        c_s[j % 4, 1] = denom.astype(BF16)
        to_sibling_near(j).start()

    def write(j):
        rows = pl.ds(pl.multiple_of(j * ROWS, ROWS), ROWS)
        return pltpu.make_async_copy(acc.at[j % 2, pl.ds(0, ROWS)], out.at[rows], out_sem.at[j % 2])

    def settle(j, swapped):
        numer, denom = both_sums(core, j, swapped)
        to_sibling_near(j).wait_recv()
        numer = numer + c_r[j, 0].astype(F32)
        denom = denom + c_r[j, 1].astype(F32)
        if not swapped:
            to_partner(j - SWAPPED).wait_recv()
            numer = numer + y_n[j - SWAPPED].astype(F32)

        @pl.when(j >= 2)
        def _():
            write(j - 2).wait()

        acc[j % 2, pl.ds(0, ROWS)] = numer / jnp.maximum(denom, 0.02)
        write(j).start()

    def each(fn, first, last, swapped):
        def body(j, carry):
            fn(j, swapped)
            return carry

        lax.fori_loop(first, last, body, 0)

    def weights_in(n, carry):
        weights_over(n).wait_recv()
        return carry

    forward(ALL)
    landed(4, ALL - 4)
    forward(ALL + 1)
    landed(4, ALL - 3)
    resid_over.wait_recv()
    lax.fori_loop(0, 2 * SWAPPED, weights_in, 0)
    each(pass_on, 0, SWAPPED, True)
    each(settle, 0, SWAPPED, True)

    def pass_on_landed(j, swapped):
        @pl.when(j == 4)
        def _():
            forward(ALL + 2)
            landed(4, ALL - 2)

        @pl.when(j == 6)
        def _():
            landed(4, ALL - 1)

        pass_on(j, swapped)

    each(pass_on_landed, SWAPPED, BLOCKS, False)
    each(settle, SWAPPED, BLOCKS, False)

    resid_over.wait_send()

    def finish(j, carry):
        to_partner(j).wait_send()
        return carry

    lax.fori_loop(0, SENT, finish, 0)

    def finish_near(j, carry):
        to_sibling_near(j).wait_send()
        return carry

    lax.fori_loop(BLOCKS - 4, BLOCKS, finish_near, 0)

    def finish_weights(n, carry):
        weights_over(n).wait_send()
        return carry

    lax.fori_loop(0, 2 * SWAPPED, finish_weights, 0)

    def finish_gather(k, carry):
        for step in range(1, 5):
            sent(step, k)

        @pl.when(k < CHUNKS)
        def _():
            swap(k, y_hi).wait_send()

        @pl.when((k < CHUNKS) & (k // EXTRA == 1 - y_lo))
        def _():
            for piece in range(2):
                extra(k, piece).wait_send()

        return carry

    lax.fori_loop(0, ALL, finish_gather, 0)
    write(BLOCKS - 2).wait()
    write(BLOCKS - 1).wait()


def shards(tokens, weights, targets, live):
    dma = pltpu.SemaphoreType.DMA
    any_space = pl.BlockSpec(memory_space=pl.ANY)
    return pl.pallas_call(
        kernel,
        out_shape=jax.ShapeDtypeStruct((QUARTER, COLS), F32),
        in_specs=[pl.BlockSpec(memory_space=pltpu.SMEM), any_space, any_space, any_space],
        out_specs=any_space,
        scratch_shapes=[
            pltpu.VMEM((ALL, 2, 4, 2, 4, 16, CHUNK), BF16),
            pltpu.VMEM((2, D, COLS), BF16),
            pltpu.VMEM((2 * SWAPPED, 2, ROWS, COLS), BF16),
            pltpu.VMEM((2, TOK, COLS), F32),
            pltpu.VMEM((2, TOK, COLS), BF16),
            pltpu.VMEM((2, TOK, COLS), BF16),
            pltpu.VMEM((SENT, ROWS, COLS), BF16),
            pltpu.VMEM((SENT, ROWS, COLS), BF16),
            pltpu.VMEM((4, 2, ROWS, COLS), BF16),
            pltpu.VMEM((BLOCKS, 2, ROWS, COLS), BF16),
            dma((CHUNKS + 3,)),
            dma((5, ALL, 4)),
            dma((5, ALL, 4)),
            dma((2 * SWAPPED,)),
            dma((2 * SWAPPED,)),
            dma((1,)),
            dma((1,)),
            dma((SENT,)),
            dma((SENT,)),
            dma((SENT,)),
            dma((SENT,)),
            dma((BLOCKS,)),
            dma((BLOCKS,)),
            dma((2,)),
        ],
        compiler_params=pltpu.CompilerParams(
            collective_id=0, has_side_effects=True, vmem_limit_bytes=60 << 20
        ),
        cost_estimate=pl.CostEstimate(
            flops=3 * 2 * 2 * TOK * D * COLS, bytes_accessed=22 << 20, transcendentals=0
        ),
        name="merge",
    )(live, tokens, weights, targets)


def solution(mesh):
    in_specs = (
        P("member", "fsdp", None),
        P("member", None, "fsdp"),
        P("member", None, "fsdp"),
        P("member"),
    )
    out_specs = P("member", "fsdp")
    return jax.shard_map(shards, mesh=mesh, in_specs=in_specs, out_specs=out_specs, check_vma=False)
```

time: 210 us -> 174 us (0.83)
  Pallas kernels: 205 us -> 168 us
    pallas_call x1, Pallas kernels: 205 us -> 168 us  [shards(): pl.pallas_call(kernel, out_shape=jax.ShapeDtypeStruct((QUARTER, COLS), F3...]
where the time goes in v2:
time: 174 us; the launch traced here: 172 us
  Pallas kernels  168 us (97%)
  local copies, waits for them, and re-layouts  4.64 us (3%)
    pallas_call x1, Pallas kernels, shards(): pl.pallas_call(kernel, out_shape=jax.ShapeDtypeStruct((QUARTER, COLS), F3...  168 us
    unnamed x1, local copies, waits for them, and re-layouts  4.64 us

profile of v2, /device:TPU:1, one launch (start us, length us, event | category | flops | bytes accessed | tf_op | source)
XLA Modules:
  0.0 172.2 jit_solution(17882215029583576198)
XLA Ops:
  0.0 167.5 %merge.1 = f32[2048,512]{1,0:T(8,128)} custom-call(s32[2]{0:T(128)} %live.1, bf16[2,16,8192]{2,1,0:T(8,128)(2,1)} %tok.1, bf16[2,8192,512]{2,1,0:T(8,128)(2,1)} %wts.1, bf16[2,512,512]{2,1,0:T(8,128)(2,1)} %tgt.1), custom_call_target="tpu_custom_call" | custom-call | flops 25769803776 | bytes 23068672 | tf_op jit(solution)/shard_map/merge/pallas_call | solution.py:378
  167.5 4.6 %copy.6 = f32[2048,512]{1,0:T(8,128)} copy(f32[2048,512]{1,0:T(8,128)} %merge.1) | data formatting | bytes 8388608

commit v3 on v2

v3 whole, which is shorter than its diff:
```python
import jax
import jax.numpy as jnp
from jax import lax
from jax.experimental import pallas as pl
from jax.experimental.pallas import tpu as pltpu
from jax.sharding import PartitionSpec as P

MESH = pl.DeviceIdType.MESH
D = 8192
SCALE = D ** (-0.5)
TOK = 512
COLS = 512
LANES = 1024
HALF = D // 2
GROUPS = 4
CHUNKS = 2 * GROUPS
EXTRA = 4
WHOLE = 2
GAP = 2
FIRST = CHUNKS + GAP
LAST = FIRST + EXTRA - WHOLE
ROWS = 256
QUARTER = D // 4
BLOCKS = QUARTER // ROWS
SWAPPED = 3
SENT = BLOCKS - SWAPPED
F32, BF16 = jnp.float32, jnp.bfloat16


def kernel(
    live, tok, wts, tgt, out,
    xg, wv, wp, acc, resid, resid_p, r_n, y_n, c_s, c_r,
    load_sem, g_send, g_recv, a_send, a_recv, w_send, w_recv, p_send, p_recv, s_send, s_recv,
    y_send, y_recv, c_send, c_recv, out_sem,
):
    member = lax.axis_index("member")
    fsdp = lax.axis_index("fsdp")
    y_lo, core = member // 2, member % 2
    x, y_hi, z = fsdp // 8, (fsdp // 4) % 2, fsdp % 4
    xl, xr = (x + 3) % 4, (x + 1) % 4
    zl, zr = (z + 3) % 4, (z + 1) % 4
    x2, z2 = (x + 2) % 4, (z + 2) % 4
    to_xr, to_xl = (member, xr * 8 + y_hi * 4 + z), (member, xl * 8 + y_hi * 4 + z)
    to_zr, to_zl = (member, x * 8 + y_hi * 4 + zr), (member, x * 8 + y_hi * 4 + zl)
    to_hi = (member, x * 8 + (1 - y_hi) * 4 + z)
    to_core = (y_lo * 2 + 1 - core, fsdp)
    to_y = ((1 - y_lo) * 2 + core, fsdp)
    to_alt = ((1 - y_lo) * 2 + core, x * 8 + (1 - y_hi) * 4 + z)

    def half_base(c):
        return (y_lo * c + (1 - y_lo) * (1 - c)) * HALF

    for k in range(GROUPS):
        for q in range(4):
            columns = pl.ds(pl.multiple_of(half_base(k % 2) + q * LANES, LANES), LANES)
            pltpu.make_async_copy(
                tok.at[k // 2, :, columns], xg.at[k, q // 2, x, q % 2, z], load_sem.at[0]
            ).start()
    load_w = pltpu.make_async_copy(wts, wv, load_sem.at[1])
    load_w.start()
    for t in range(2):
        for hg in range(2):
            rows_of = y_hi + hg - 2 * y_hi * hg
            for xx in range(4):
                pltpu.make_async_copy(
                    tgt.at[t, xx, rows_of], c_s.at[t, hg, pl.ds(xx * 64, 64)], load_sem.at[2]
                ).start()

    barrier = pltpu.get_barrier_semaphore()
    for peer in (to_xr, to_xl, to_zr, to_zl, to_hi, to_core, to_y, to_alt):
        pl.semaphore_signal(barrier, inc=1, device_id=peer, device_id_type=MESH)
    pl.semaphore_wait(barrier, 8)

    def remote(src, dst, send, recv, peer):
        return pltpu.make_async_remote_copy(
            src_ref=src, dst_ref=dst, send_sem=send, recv_sem=recv, device_id=peer, device_id_type=MESH
        )

    def swap(k):
        return remote(
            xg.at[k, :, x, :, z], xg.at[k + 4, :, x, :, z], g_send.at[0, k, 0], g_recv.at[0, k + 4, 0], to_hi
        )

    def seed(k):
        part = xg.at[k, :, x, :, z]
        return remote(part, part, g_send.at[0, k, 0], g_recv.at[0, k, 0], to_hi)

    def extra_seed(e, group, quarter):
        src = xg.at[2 * group, quarter, x, e // 2, z, :, pl.ds((e % 2) * 512, 512)]
        dst = xg.at[CHUNKS + e, group % 2, x, 1 - group // 2, z, :, pl.ds(quarter * 512, 512)]
        return remote(src, dst, g_send.at[0, CHUNKS + e, 0], g_recv.at[0, CHUNKS + e, 0], to_alt)

    def extra_whole(e, group, quarter):
        src = xg.at[2 * group, quarter, :, e // 2, :, :, pl.ds((e % 2) * 512, 512)]
        dst = xg.at[CHUNKS + e, group % 2, :, 1 - group // 2, :, :, pl.ds(quarter * 512, 512)]
        return remote(src, dst, a_send.at[e, group], a_recv.at[e, group], to_alt)

    def extra_whole_all(e, group):
        part = xg.at[CHUNKS + e, group % 2, :, 1 - group // 2]
        return remote(part, part, a_send.at[e, group], a_recv.at[e, group], to_alt)

    def hops(step, k):
        if step == 1:
            mine = [xg.at[k, q, x, :, z] for q in range(2)]
            return [
                (mine[0], to_xr, xg.at[k, 0, xl, :, z]),
                (mine[0], to_xl, xg.at[k, 0, xr, :, z]),
                (mine[1], to_zr, xg.at[k, 1, x, :, zl]),
                (mine[1], to_zl, xg.at[k, 1, x, :, zr]),
            ]
        if step == 2:
            return [
                (xg.at[k, 0, xl, 0, z], to_xr, xg.at[k, 0, x2, 0, z]),
                (xg.at[k, 0, xr, 1, z], to_xl, xg.at[k, 0, x2, 1, z]),
                (xg.at[k, 1, x, 0, zl], to_zr, xg.at[k, 1, x, 0, z2]),
                (xg.at[k, 1, x, 1, zr], to_zl, xg.at[k, 1, x, 1, z2]),
            ]
        if step == 3:
            return [
                (xg.at[k, 0, :, :, z], to_zr, xg.at[k, 0, :, :, zl]),
                (xg.at[k, 0, :, :, z], to_zl, xg.at[k, 0, :, :, zr]),
                (xg.at[k, 1, x], to_xr, xg.at[k, 1, xl]),
                (xg.at[k, 1, x], to_xl, xg.at[k, 1, xr]),
            ]
        return [
            (xg.at[k, 0, :, 0, zl], to_zr, xg.at[k, 0, :, 0, z2]),
            (xg.at[k, 0, :, 1, zr], to_zl, xg.at[k, 0, :, 1, z2]),
            (xg.at[k, 1, xl, 0], to_xr, xg.at[k, 1, x2, 0]),
            (xg.at[k, 1, xr, 1], to_xl, xg.at[k, 1, x2, 1]),
        ]

    def start(step, k):
        for i, (src, peer, _) in enumerate(hops(step, k)):
            remote(src, src, g_send.at[step, k, i], g_recv.at[step, k, i], peer).start()

    def landed(step, k):
        for i, (_, peer, dst) in enumerate(hops(step, k)):
            remote(dst, dst, g_send.at[step, k, i], g_recv.at[step, k, i], peer).wait_recv()

    def sent(step, k):
        for i, (src, peer, _) in enumerate(hops(step, k)):
            remote(src, src, g_send.at[step, k, i], g_recv.at[step, k, i], peer).wait_send()

    def weights_over(n):
        quarter, j = n % 2, n // 2
        rows = pl.ds(pl.multiple_of((1 - y_lo) * HALF + quarter * QUARTER + j * ROWS, ROWS), ROWS)
        return remote(wts.at[:, rows], wp.at[n], w_send.at[n], w_recv.at[n], to_y)

    def resid_over(g):
        part = (g % 2, g // 2)
        return remote(resid.at[part], resid_p.at[part], p_send.at[g], p_recv.at[g], to_y)

    def chunk_at(p):
        return ((p >= 0) & (p < CHUNKS)) | ((p >= FIRST) & (p < LAST)), jnp.where(p < CHUNKS, p, p - GAP + WHOLE)

    def forward(i):
        for step in (4, 3, 2):
            valid, k = chunk_at(i - step + 1)

            @pl.when(valid)
            def _():
                landed(step - 1, k)
                start(step, k)

    def begin(i):
        valid, k = chunk_at(i)

        @pl.when(valid)
        def _():
            @pl.when(k >= GROUPS)
            def _():
                seed(k).wait_recv()

            start(1, k)

    pltpu.make_async_copy(tok, tok, load_sem.at[0]).wait()
    start(1, 0)
    for k in range(GROUPS):
        swap(k).start()
    acc[...] = jnp.zeros_like(acc)
    load_w.wait()
    pltpu.make_async_copy(c_s.at[pl.ds(0, 2)], c_s.at[pl.ds(0, 2)], load_sem.at[2]).wait()

    def tick(i, carry):
        forward(i)

        @pl.when(i >= 1)
        def _():
            begin(i)

        @pl.when(i == 6)
        def _():
            for e in range(WHOLE, EXTRA):
                for group in range(GROUPS):
                    for quarter in range(2):
                        extra_seed(e, group, quarter).start()

        @pl.when((i >= 2) & (i < 2 + 2 * SWAPPED))
        def _():
            weights_over(i - 2).start()

        k = i - 4

        @pl.when(k >= 0)
        def _():
            group = k // 2
            t, hg = group % 2, group // 2
            landed(4, k)

            @pl.when(k % 2 == 0)
            def _():
                for e in range(WHOLE):
                    for quarter in range(2):
                        extra_whole(e, group, quarter).start()

            for q in range(4):
                rows = pl.ds(pl.multiple_of(half_base(k % 2) + q * LANES, LANES), LANES)
                part = xg[k, q // 2, :, q % 2].reshape(TOK // 2, LANES)
                acc[t, hg] += jnp.dot(part, wv[t, rows, :], preferred_element_type=F32)

            @pl.when(k % 2 == 1)
            def _():
                at = lax.broadcasted_iota(jnp.int32, (TOK // 2, COLS), 0)
                row_ids = (at // 64) * 128 + at % 64 + (y_hi + hg - 2 * y_hi * hg) * 64
                diff = acc[t, hg] * SCALE - c_s[t, hg].astype(F32)
                resid[t, hg] = jnp.where(row_ids < live[t], diff, 0.0).astype(BF16)
                resid_over(group).start()

        return carry

    lax.fori_loop(0, CHUNKS + 4, tick, 0)

    def fisher_of(first, second, res):
        inputs = jnp.concatenate(
            [first.reshape(TOK // 2, ROWS), second.reshape(TOK // 2, ROWS)], axis=0
        )
        grad = SCALE * lax.dot_general(
            inputs, res.reshape(TOK, COLS), (((0,), (0,)), ((), ())), preferred_element_type=F32
        )
        return grad * grad

    def own_sums(c, quarter, j, with_denom=True):
        columns = pl.ds(pl.multiple_of((j % 4) * ROWS, ROWS), ROWS)
        rows = pl.ds(pl.multiple_of(half_base(c) + quarter * QUARTER + j * ROWS, ROWS), ROWS)
        numer = denom = None
        for t in range(2):
            parts = [xg[2 * (2 * hg + t) + c, quarter, :, j // 4, :, :, columns] for hg in range(2)]
            fisher = fisher_of(*parts, resid[t])
            term = fisher * wv[t, rows, :].astype(F32)
            numer = term if t == 0 else numer + term
            if with_denom:
                denom = fisher if t == 0 else denom + fisher
        return numer, denom

    def to_sibling(i):
        return remote(c_s.at[i // 2, i % 2], r_n.at[i], s_send.at[i], s_recv.at[i], to_core)

    def to_partner(i):
        return remote(r_n.at[i], y_n.at[i], y_send.at[i], y_recv.at[i], to_y)

    def outward(i, carry):
        @pl.when(i < SENT)
        def _():
            c_s[i // 2, i % 2] = own_sums(0, 1 - core, SWAPPED + i, False)[0].astype(BF16)
            to_sibling(i).start()

        @pl.when(i >= 1)
        def _():
            n = i - 1
            numer, _ = own_sums(0, core, SWAPPED + n, False)
            to_sibling(n).wait_recv()
            r_n[n] = (numer + r_n[n].astype(F32)).astype(BF16)
            to_partner(n).start()

        return carry

    forward(CHUNKS + 4)
    lax.fori_loop(0, SENT + 1, outward, 0)

    def both_sums(quarter, j, swapped):
        numer, denom = own_sums(1, quarter, j)
        columns = pl.ds(pl.multiple_of(quarter * 512 + (j % 2) * ROWS, ROWS), ROWS)
        for t in range(2):
            parts = [xg[CHUNKS + j // 2, t, :, hg, :, :, columns] for hg in range(2)]
            fisher = fisher_of(*parts, resid_p[t])
            if swapped:
                numer = numer + fisher * wp[2 * j + quarter, t].astype(F32)
            denom = denom + fisher
        return numer, denom

    def to_sibling_near(j):
        return remote(c_s.at[j % 4], c_r.at[j], c_send.at[j], c_recv.at[j], to_core)

    def left_sibling(i, carry):
        to_sibling(i).wait_send()
        return carry

    def pass_on(j, swapped):
        numer, denom = both_sums(1 - core, j, swapped)

        @pl.when(j >= 4)
        def _():
            to_sibling_near(j - 4).wait_send()

        @pl.when(j == 0)
        def _():
            lax.fori_loop(0, SENT, left_sibling, 0)

        c_s[j % 4, 0] = numer.astype(BF16)
        c_s[j % 4, 1] = denom.astype(BF16)
        to_sibling_near(j).start()

    def write(j):
        rows = pl.ds(pl.multiple_of(j * ROWS, ROWS), ROWS)
        return pltpu.make_async_copy(acc.at[j % 2, 0], out.at[rows], out_sem.at[j % 2])

    def settle(j, swapped):
        numer, denom = both_sums(core, j, swapped)
        to_sibling_near(j).wait_recv()
        numer = numer + c_r[j, 0].astype(F32)
        denom = denom + c_r[j, 1].astype(F32)
        if not swapped:
            to_partner(j - SWAPPED).wait_recv()
            numer = numer + y_n[j - SWAPPED].astype(F32)

        @pl.when(j >= 2)
        def _():
            write(j - 2).wait()

        acc[j % 2, 0] = numer / jnp.maximum(denom, 0.02)
        write(j).start()

    def each(fn, first, last, swapped):
        def body(j, carry):
            fn(j, swapped)
            return carry

        lax.fori_loop(first, last, body, 0)

    def weights_in(n, carry):
        weights_over(n).wait_recv()
        return carry

    for i in range(CHUNKS + 5, LAST + 3):
        forward(i)
    for g in range(GROUPS):
        resid_over(g).wait_recv()
    for e in range(WHOLE):
        for group in range(GROUPS):
            extra_whole_all(e, group).wait_recv()
    lax.fori_loop(0, 2 * SWAPPED, weights_in, 0)
    each(pass_on, 0, SWAPPED, True)
    each(settle, 0, SWAPPED, True)

    def pass_on_landed(j, swapped):
        for e in range(WHOLE, EXTRA):

            @pl.when(j == 2 * e)
            def _():
                landed(4, CHUNKS + e)

        pass_on(j, swapped)

    each(pass_on_landed, SWAPPED, BLOCKS, False)
    each(settle, SWAPPED, BLOCKS, False)

    for g in range(GROUPS):
        resid_over(g).wait_send()

    def finish(j, carry):
        to_partner(j).wait_send()
        return carry

    lax.fori_loop(0, SENT, finish, 0)

    def finish_near(j, carry):
        to_sibling_near(j).wait_send()
        return carry

    lax.fori_loop(BLOCKS - 4, BLOCKS, finish_near, 0)

    def finish_weights(n, carry):
        weights_over(n).wait_send()
        return carry

    lax.fori_loop(0, 2 * SWAPPED, finish_weights, 0)

    for k in range(GROUPS):
        swap(k).wait_send()
    for e in range(WHOLE):
        for group in range(GROUPS):
            extra_whole_all(e, group).wait_send()
    for e in range(WHOLE, EXTRA):
        seed(CHUNKS + e).wait_send()

    def finish_gather(k, carry):
        for step in range(1, 5):
            sent(step, k)
        return carry

    lax.fori_loop(0, CHUNKS, finish_gather, 0)
    lax.fori_loop(CHUNKS + WHOLE, CHUNKS + EXTRA, finish_gather, 0)
    write(BLOCKS - 2).wait()
    write(BLOCKS - 1).wait()


def shards(tokens, weights, targets, live):
    dma = pltpu.SemaphoreType.DMA
    any_space = pl.BlockSpec(memory_space=pl.ANY)
    return pl.pallas_call(
        kernel,
        out_shape=jax.ShapeDtypeStruct((QUARTER, COLS), F32),
        in_specs=[pl.BlockSpec(memory_space=pltpu.SMEM), any_space, any_space, any_space],
        out_specs=any_space,
        scratch_shapes=[
            pltpu.VMEM((CHUNKS + EXTRA, 2, 4, 2, 4, 16, LANES), BF16),
            pltpu.VMEM((2, D, COLS), BF16),
            pltpu.VMEM((2 * SWAPPED, 2, ROWS, COLS), BF16),
            pltpu.VMEM((2, 2, TOK // 2, COLS), F32),
            pltpu.VMEM((2, 2, TOK // 2, COLS), BF16),
            pltpu.VMEM((2, 2, TOK // 2, COLS), BF16),
            pltpu.VMEM((SENT, ROWS, COLS), BF16),
            pltpu.VMEM((SENT, ROWS, COLS), BF16),
            pltpu.VMEM((4, 2, ROWS, COLS), BF16),
            pltpu.VMEM((BLOCKS, 2, ROWS, COLS), BF16),
            dma((3,)),
            dma((5, CHUNKS + EXTRA, 4)),
            dma((5, CHUNKS + EXTRA, 4)),
            dma((WHOLE, GROUPS)),
            dma((WHOLE, GROUPS)),
            dma((2 * SWAPPED,)),
            dma((2 * SWAPPED,)),
            dma((GROUPS,)),
            dma((GROUPS,)),
            dma((SENT,)),
            dma((SENT,)),
            dma((SENT,)),
            dma((SENT,)),
            dma((BLOCKS,)),
            dma((BLOCKS,)),
            dma((2,)),
        ],
        compiler_params=pltpu.CompilerParams(
            collective_id=0, has_side_effects=True, vmem_limit_bytes=60 << 20
        ),
        cost_estimate=pl.CostEstimate(
            flops=3 * 2 * 2 * TOK * D * COLS, bytes_accessed=22 << 20, transcendentals=0
        ),
        name="merge",
    )(live, tokens, weights, targets.reshape(2, 4, 2, 64, COLS))


def solution(mesh):
    in_specs = (
        P("member", "fsdp", None),
        P("member", None, "fsdp"),
        P("member", None, "fsdp"),
        P("member"),
    )
    out_specs = P("member", "fsdp")
    return jax.shard_map(shards, mesh=mesh, in_specs=in_specs, out_specs=out_specs, check_vma=False)
```

time: 174 us -> 160 us (0.920)
  Pallas kernels: 168 us -> 155 us
    pallas_call x1, Pallas kernels: 168 us -> 155 us  [shards(): pl.pallas_call(kernel, out_shape=jax.ShapeDtypeStruct((QUARTER, COLS), F3...]
where the time goes in v3:
time: 160 us
  Pallas kernels  155 us (97%)
  local copies, waits for them, and re-layouts  4.64 us (3%)
    pallas_call x1, Pallas kernels, shards(): pl.pallas_call(kernel, out_shape=jax.ShapeDtypeStruct((QUARTER, COLS), F3...  155 us
    unnamed x1, local copies, waits for them, and re-layouts  4.64 us

profile of v3, /device:TPU:1, one launch (start us, length us, event | category | flops | bytes accessed | tf_op | source)
XLA Modules:
  0.0 159.7 jit_solution(12804930530849577307)
XLA Ops:
  0.0 155.1 %merge.1 = f32[2048,512]{1,0:T(8,128)} custom-call(s32[2]{0:T(128)} %live.1, bf16[2,16,8192]{2,1,0:T(8,128)(2,1)} %tok.1, bf16[2,8192,512]{2,1,0:T(8,128)(2,1)} %wts.1, bf16[2,4,2,64,512]{4,3,2,1,0:T(8,128)(2,1)} %bitcast.1), custom_call_target="tpu_custom_call" | custom-call | flops 25769803776 | bytes 23068672 | tf_op jit(solution)/shard_map/merge/pallas_call | solution.py:410
  155.1 4.6 %copy.6 = f32[2048,512]{1,0:T(8,128)} copy(f32[2048,512]{1,0:T(8,128)} %merge.1) | data formatting | bytes 8388608

commit v4 on v3

--- a/solution.py
+++ b/solution.py
@@ -15,7 +15,7 @@
 GROUPS = 4
 CHUNKS = 2 * GROUPS
 EXTRA = 4
-WHOLE = 2
+WHOLE = 1
 GAP = 2
 FIRST = CHUNKS + GAP
 LAST = FIRST + EXTRA - WHOLE
@@ -154,39 +154,29 @@
         return ((p >= 0) & (p < CHUNKS)) | ((p >= FIRST) & (p < LAST)), jnp.where(p < CHUNKS, p, p - GAP + WHOLE)
 
     def forward(i):
-        for step in (4, 3, 2):
+        for step in (3, 2, 1, 4):
             valid, k = chunk_at(i - step + 1)
 
             @pl.when(valid)
             def _():
-                landed(step - 1, k)
+                if step > 1:
+                    landed(step - 1, k)
+                else:
+
+                    @pl.when(k >= GROUPS)
+                    def _():
+                        seed(k).wait_recv()
+
                 start(step, k)
-
-    def begin(i):
-        valid, k = chunk_at(i)
-
-        @pl.when(valid)
-        def _():
-            @pl.when(k >= GROUPS)
-            def _():
-                seed(k).wait_recv()
-
-            start(1, k)
 
     pltpu.make_async_copy(tok, tok, load_sem.at[0]).wait()
     start(1, 0)
     for k in range(GROUPS):
         swap(k).start()
     acc[...] = jnp.zeros_like(acc)
-    load_w.wait()
-    pltpu.make_async_copy(c_s.at[pl.ds(0, 2)], c_s.at[pl.ds(0, 2)], load_sem.at[2]).wait()
 
     def tick(i, carry):
         forward(i)
-
-        @pl.when(i >= 1)
-        def _():
-            begin(i)
 
         @pl.when(i == 6)
         def _():
@@ -206,6 +196,11 @@
             group = k // 2
             t, hg = group % 2, group // 2
             landed(4, k)
+
+            @pl.when(k == 0)
+            def _():
+                load_w.wait()
+                pltpu.make_async_copy(c_s.at[pl.ds(0, 2)], c_s.at[pl.ds(0, 2)], load_sem.at[2]).wait()
 
             @pl.when(k % 2 == 0)
             def _():
@@ -228,7 +223,7 @@
 
         return carry
 
-    lax.fori_loop(0, CHUNKS + 4, tick, 0)
+    lax.fori_loop(1, CHUNKS + 4, tick, 0)
 
     def fisher_of(first, second, res):
         inputs = jnp.concatenate(
@@ -330,39 +325,41 @@
         acc[j % 2, 0] = numer / jnp.maximum(denom, 0.02)
         write(j).start()
 
-    def each(fn, first, last, swapped):
-        def body(j, carry):
-            fn(j, swapped)
-            return carry
-
-        lax.fori_loop(first, last, body, 0)
-
     def weights_in(n, carry):
         weights_over(n).wait_recv()
         return carry
 
-    for i in range(CHUNKS + 5, LAST + 3):
-        forward(i)
+    forward(CHUNKS + 5)
     for g in range(GROUPS):
         resid_over(g).wait_recv()
     for e in range(WHOLE):
         for group in range(GROUPS):
             extra_whole_all(e, group).wait_recv()
     lax.fori_loop(0, 2 * SWAPPED, weights_in, 0)
-    each(pass_on, 0, SWAPPED, True)
-    each(settle, 0, SWAPPED, True)
-
-    def pass_on_landed(j, swapped):
-        for e in range(WHOLE, EXTRA):
-
-            @pl.when(j == 2 * e)
-            def _():
-                landed(4, CHUNKS + e)
-
-        pass_on(j, swapped)
-
-    each(pass_on_landed, SWAPPED, BLOCKS, False)
-    each(settle, SWAPPED, BLOCKS, False)
+
+    def near(first, last, swapped):
+        def body(j, carry):
+            @pl.when(j > first)
+            def _():
+                settle(j - 1, swapped)
+
+            for e in range(WHOLE, EXTRA):
+
+                @pl.when((j == 2 * e) & (j < last))
+                def _():
+                    forward(CHUNKS + 6 + e - WHOLE)
+                    landed(4, CHUNKS + e)
+
+            @pl.when(j < last)
+            def _():
+                pass_on(j, swapped)
+
+            return carry
+
+        lax.fori_loop(first, last + 1, body, 0)
+
+    near(0, SWAPPED, True)
+    near(SWAPPED, BLOCKS, False)
 
     for g in range(GROUPS):
         resid_over(g).wait_send()

time: 160 us -> 152 us (0.950)
  Pallas kernels: 155 us -> 147 us
    pallas_call x1, Pallas kernels: 155 us -> 147 us  [shards(): pl.pallas_call(kernel, out_shape=jax.ShapeDtypeStruct((QUARTER, COLS), F3...]
where the time goes in v4:
time: 152 us
  Pallas kernels  147 us (97%)
  local copies, waits for them, and re-layouts  4.64 us (3%)
    pallas_call x1, Pallas kernels, shards(): pl.pallas_call(kernel, out_shape=jax.ShapeDtypeStruct((QUARTER, COLS), F3...  147 us
    unnamed x1, local copies, waits for them, and re-layouts  4.64 us

profile of v4, /device:TPU:1, one launch (start us, length us, event | category | flops | bytes accessed | tf_op | source)
XLA Modules:
  0.0 151.7 jit_solution(12990464872484674185)
XLA Ops:
  0.0 147.1 %merge.1 = f32[2048,512]{1,0:T(8,128)} custom-call(s32[2]{0:T(128)} %live.1, bf16[2,16,8192]{2,1,0:T(8,128)(2,1)} %tok.1, bf16[2,8192,512]{2,1,0:T(8,128)(2,1)} %wts.1, bf16[2,4,2,64,512]{4,3,2,1,0:T(8,128)(2,1)} %bitcast.1), custom_call_target="tpu_custom_call" | custom-call | flops 25769803776 | bytes 23068672 | tf_op jit(solution)/shard_map/merge/pallas_call | solution.py:407
  147.1 4.6 %copy.6 = f32[2048,512]{1,0:T(8,128)} copy(f32[2048,512]{1,0:T(8,128)} %merge.1) | data formatting | bytes 8388608

commit v5 on v4

--- a/solution.py
+++ b/solution.py
@@ -16,20 +16,22 @@
 CHUNKS = 2 * GROUPS
 EXTRA = 4
 WHOLE = 1
-GAP = 2
-FIRST = CHUNKS + GAP
-LAST = FIRST + EXTRA - WHOLE
+E0, E1, E2 = range(CHUNKS + WHOLE, CHUNKS + EXTRA)
 ROWS = 256
 QUARTER = D // 4
 BLOCKS = QUARTER // ROWS
-SWAPPED = 3
+SWAPPED = 2
+PART = 128
+OVER = 2 * (SWAPPED + 1)
 SENT = BLOCKS - SWAPPED
+ZERO = 2 * OVER
+NUMER = ZERO + 2
 F32, BF16 = jnp.float32, jnp.bfloat16
 
 
 def kernel(
     live, tok, wts, tgt, out,
-    xg, wv, wp, acc, resid, resid_p, r_n, y_n, c_s, c_r,
+    xg, wv, wy, acc, resid, resid_p, r_n, c_s, c_r,
     load_sem, g_send, g_recv, a_send, a_recv, w_send, w_recv, p_send, p_recv, s_send, s_recv,
     y_send, y_recv, c_send, c_recv, out_sem,
 ):
@@ -50,25 +52,17 @@
     def half_base(c):
         return (y_lo * c + (1 - y_lo) * (1 - c)) * HALF
 
+    barrier = pltpu.get_barrier_semaphore()
+    for peer in (to_xr, to_xl, to_zr, to_zl, to_hi, to_core, to_y, to_alt):
+        pl.semaphore_signal(barrier, inc=1, device_id=peer, device_id_type=MESH)
+
     for k in range(GROUPS):
         for q in range(4):
             columns = pl.ds(pl.multiple_of(half_base(k % 2) + q * LANES, LANES), LANES)
             pltpu.make_async_copy(
-                tok.at[k // 2, :, columns], xg.at[k, q // 2, x, q % 2, z], load_sem.at[0]
+                tok.at[k // 2, :, columns], xg.at[k, q // 2, x, q % 2, z], load_sem.at[0 if k == 0 else 3]
             ).start()
     load_w = pltpu.make_async_copy(wts, wv, load_sem.at[1])
-    load_w.start()
-    for t in range(2):
-        for hg in range(2):
-            rows_of = y_hi + hg - 2 * y_hi * hg
-            for xx in range(4):
-                pltpu.make_async_copy(
-                    tgt.at[t, xx, rows_of], c_s.at[t, hg, pl.ds(xx * 64, 64)], load_sem.at[2]
-                ).start()
-
-    barrier = pltpu.get_barrier_semaphore()
-    for peer in (to_xr, to_xl, to_zr, to_zl, to_hi, to_core, to_y, to_alt):
-        pl.semaphore_signal(barrier, inc=1, device_id=peer, device_id_type=MESH)
     pl.semaphore_wait(barrier, 8)
 
     def remote(src, dst, send, recv, peer):
@@ -143,40 +137,70 @@
 
     def weights_over(n):
         quarter, j = n % 2, n // 2
-        rows = pl.ds(pl.multiple_of((1 - y_lo) * HALF + quarter * QUARTER + j * ROWS, ROWS), ROWS)
-        return remote(wts.at[:, rows], wp.at[n], w_send.at[n], w_recv.at[n], to_y)
+        size = ROWS if n < 2 * SWAPPED else PART
+        rows = pl.ds(pl.multiple_of((1 - y_lo) * HALF + quarter * QUARTER + j * ROWS, ROWS), size)
+        dst = wy.at[pl.ds(2 * n, 2), pl.ds(0, size)]
+        return remote(wts.at[:, rows], dst, w_send.at[n], w_recv.at[n], to_y)
 
     def resid_over(g):
         part = (g % 2, g // 2)
         return remote(resid.at[part], resid_p.at[part], p_send.at[g], p_recv.at[g], to_y)
 
-    def chunk_at(p):
-        return ((p >= 0) & (p < CHUNKS)) | ((p >= FIRST) & (p < LAST)), jnp.where(p < CHUNKS, p, p - GAP + WHOLE)
+    def follow(step, k):
+        if step == 1:
+            seed(k).wait_recv()
+        else:
+            landed(step - 1, k)
+        start(step, k)
 
     def forward(i):
-        for step in (3, 2, 1, 4):
-            valid, k = chunk_at(i - step + 1)
-
-            @pl.when(valid)
-            def _():
-                if step > 1:
-                    landed(step - 1, k)
-                else:
-
-                    @pl.when(k >= GROUPS)
-                    def _():
-                        seed(k).wait_recv()
-
-                start(step, k)
-
-    pltpu.make_async_copy(tok, tok, load_sem.at[0]).wait()
+        for step, k in ((3, i - 2), (2, i), (1, i + 1), (4, i - 3)):
+
+            @pl.when((k >= (GROUPS if step == 1 else 0)) & (k < CHUNKS))
+            def _():
+                follow(step, k)
+
+    first = xg.at[0, :, x, :, z]
+    pltpu.make_async_copy(first, first, load_sem.at[0]).wait()
     start(1, 0)
+    others = xg.at[pl.ds(1, GROUPS - 1), :, x, :, z]
+    pltpu.make_async_copy(others, others, load_sem.at[3]).wait()
     for k in range(GROUPS):
         swap(k).start()
+    start(1, 1)
+    start(1, 2)
+    load_w.start()
+    for t in range(2):
+        for hg in range(2):
+            rows_of = y_hi + hg - 2 * y_hi * hg
+            for xx in range(4):
+                pltpu.make_async_copy(
+                    tgt.at[t, xx, rows_of], c_s.at[t, hg, pl.ds(xx * 64, 64)], load_sem.at[2]
+                ).start()
     acc[...] = jnp.zeros_like(acc)
+    nothing = jnp.zeros((ROWS, COLS), BF16)
+    for n in range(2):
+        wy[ZERO + n] = nothing
+        for t in range(2):
+            wy[2 * (2 * SWAPPED + n) + t, pl.ds(PART, ROWS - PART)] = nothing[PART:]
+    wy[NUMER, pl.ds(0, PART)] = nothing[:PART]
 
     def tick(i, carry):
         forward(i)
+
+        @pl.when(i == 0)
+        def _():
+            start(1, 3)
+
+        @pl.when(i == CHUNKS + 1)
+        def _():
+            follow(1, E0)
+
+        @pl.when(i == CHUNKS + 2)
+        def _():
+            follow(1, E1)
+            follow(1, E2)
+            follow(2, E0)
 
         @pl.when(i == 6)
         def _():
@@ -185,9 +209,11 @@
                     for quarter in range(2):
                         extra_seed(e, group, quarter).start()
 
-        @pl.when((i >= 2) & (i < 2 + 2 * SWAPPED))
-        def _():
-            weights_over(i - 2).start()
+        for n in range(OVER):
+
+            @pl.when(i == n + 1)
+            def _():
+                weights_over(n).start()
 
         k = i - 4
 
@@ -223,7 +249,7 @@
 
         return carry
 
-    lax.fori_loop(1, CHUNKS + 4, tick, 0)
+    lax.fori_loop(0, CHUNKS + 4, tick, 0)
 
     def fisher_of(first, second, res):
         inputs = jnp.concatenate(
@@ -251,9 +277,17 @@
         return remote(c_s.at[i // 2, i % 2], r_n.at[i], s_send.at[i], s_recv.at[i], to_core)
 
     def to_partner(i):
-        return remote(r_n.at[i], y_n.at[i], y_send.at[i], y_recv.at[i], to_y)
+        return remote(r_n.at[i], wy.at[NUMER + i], y_send.at[i], y_recv.at[i], to_y)
+
+    def to_partner_first():
+        rows = pl.ds(PART, ROWS - PART)
+        return remote(r_n.at[0, rows], wy.at[NUMER, rows], y_send.at[0], y_recv.at[0], to_y)
 
     def outward(i, carry):
+        @pl.when(i == 3)
+        def _():
+            follow(3, E1)
+
         @pl.when(i < SENT)
         def _():
             c_s[i // 2, i % 2] = own_sums(0, 1 - core, SWAPPED + i, False)[0].astype(BF16)
@@ -265,21 +299,30 @@
             numer, _ = own_sums(0, core, SWAPPED + n, False)
             to_sibling(n).wait_recv()
             r_n[n] = (numer + r_n[n].astype(F32)).astype(BF16)
-            to_partner(n).start()
+
+            @pl.when(n == 0)
+            def _():
+                to_partner_first().start()
+
+            @pl.when(n > 0)
+            def _():
+                to_partner(n).start()
 
         return carry
 
-    forward(CHUNKS + 4)
+    follow(2, E1)
+    follow(2, E2)
+    follow(3, E0)
     lax.fori_loop(0, SENT + 1, outward, 0)
 
-    def both_sums(quarter, j, swapped):
+    def both_sums(quarter, j):
         numer, denom = own_sums(1, quarter, j)
         columns = pl.ds(pl.multiple_of(quarter * 512 + (j % 2) * ROWS, ROWS), ROWS)
+        place = 2 * jnp.where(j <= SWAPPED, 2 * j + quarter, OVER)
         for t in range(2):
             parts = [xg[CHUNKS + j // 2, t, :, hg, :, :, columns] for hg in range(2)]
             fisher = fisher_of(*parts, resid_p[t])
-            if swapped:
-                numer = numer + fisher * wp[2 * j + quarter, t].astype(F32)
+            numer = numer + fisher * wy[place + t].astype(F32)
             denom = denom + fisher
         return numer, denom
 
@@ -290,8 +333,8 @@
         to_sibling(i).wait_send()
         return carry
 
-    def pass_on(j, swapped):
-        numer, denom = both_sums(1 - core, j, swapped)
+    def pass_on(j):
+        numer, denom = both_sums(1 - core, j)
 
         @pl.when(j >= 4)
         def _():
@@ -309,14 +352,21 @@
         rows = pl.ds(pl.multiple_of(j * ROWS, ROWS), ROWS)
         return pltpu.make_async_copy(acc.at[j % 2, 0], out.at[rows], out_sem.at[j % 2])
 
-    def settle(j, swapped):
-        numer, denom = both_sums(core, j, swapped)
+    def settle(j):
+        numer, denom = both_sums(core, j)
         to_sibling_near(j).wait_recv()
         numer = numer + c_r[j, 0].astype(F32)
         denom = denom + c_r[j, 1].astype(F32)
-        if not swapped:
+
+        @pl.when(j == SWAPPED)
+        def _():
+            to_partner_first().wait_recv()
+
+        @pl.when(j > SWAPPED)
+        def _():
             to_partner(j - SWAPPED).wait_recv()
-            numer = numer + y_n[j - SWAPPED].astype(F32)
+
+        numer = numer + wy[jnp.where(j < SWAPPED, ZERO, NUMER - SWAPPED + j)].astype(F32)
 
         @pl.when(j >= 2)
         def _():
@@ -325,78 +375,67 @@
         acc[j % 2, 0] = numer / jnp.maximum(denom, 0.02)
         write(j).start()
 
-    def weights_in(n, carry):
-        weights_over(n).wait_recv()
-        return carry
-
-    forward(CHUNKS + 5)
+    follow(4, E0)
+    follow(3, E2)
     for g in range(GROUPS):
         resid_over(g).wait_recv()
     for e in range(WHOLE):
         for group in range(GROUPS):
             extra_whole_all(e, group).wait_recv()
-    lax.fori_loop(0, 2 * SWAPPED, weights_in, 0)
-
-    def near(first, last, swapped):
-        def body(j, carry):
-            @pl.when(j > first)
-            def _():
-                settle(j - 1, swapped)
-
-            for e in range(WHOLE, EXTRA):
-
-                @pl.when((j == 2 * e) & (j < last))
-                def _():
-                    forward(CHUNKS + 6 + e - WHOLE)
-                    landed(4, CHUNKS + e)
-
-            @pl.when(j < last)
-            def _():
-                pass_on(j, swapped)
-
-            return carry
-
-        lax.fori_loop(first, last + 1, body, 0)
-
-    near(0, SWAPPED, True)
-    near(SWAPPED, BLOCKS, False)
-
+    for n in range(OVER):
+        weights_over(n).wait_recv()
+
+    def left_gather(k, carry):
+        for step in range(1, 5):
+            sent(step, k)
+        return carry
+
+    lax.fori_loop(0, CHUNKS, left_gather, 0)
+    for k in range(GROUPS):
+        swap(k).wait_send()
+    for n in range(OVER):
+        weights_over(n).wait_send()
     for g in range(GROUPS):
         resid_over(g).wait_send()
-
-    def finish(j, carry):
-        to_partner(j).wait_send()
+    for e in range(WHOLE, EXTRA):
+        seed(CHUNKS + e).wait_send()
+
+    def near(j, carry):
+        @pl.when(j >= 1)
+        def _():
+            settle(j - 1)
+
+        @pl.when(j == 2)
+        def _():
+            follow(4, E1)
+            landed(4, E0)
+
+        @pl.when(j == 4)
+        def _():
+            follow(4, E2)
+            landed(4, E1)
+
+        @pl.when(j == 6)
+        def _():
+            landed(4, E2)
+
+        @pl.when(j < BLOCKS)
+        def _():
+            pass_on(j)
+
         return carry
 
-    lax.fori_loop(0, SENT, finish, 0)
-
-    def finish_near(j, carry):
-        to_sibling_near(j).wait_send()
-        return carry
-
-    lax.fori_loop(BLOCKS - 4, BLOCKS, finish_near, 0)
-
-    def finish_weights(n, carry):
-        weights_over(n).wait_send()
-        return carry
-
-    lax.fori_loop(0, 2 * SWAPPED, finish_weights, 0)
-
-    for k in range(GROUPS):
-        swap(k).wait_send()
+    lax.fori_loop(0, BLOCKS + 1, near, 0)
+
     for e in range(WHOLE):
         for group in range(GROUPS):
             extra_whole_all(e, group).wait_send()
-    for e in range(WHOLE, EXTRA):
-        seed(CHUNKS + e).wait_send()
-
-    def finish_gather(k, carry):
-        for step in range(1, 5):
-            sent(step, k)
-        return carry
-
-    lax.fori_loop(0, CHUNKS, finish_gather, 0)
-    lax.fori_loop(CHUNKS + WHOLE, CHUNKS + EXTRA, finish_gather, 0)
+    to_partner_first().wait_send()
+    for i in range(1, SENT):
+        to_partner(i).wait_send()
+    for j in range(BLOCKS - 4, BLOCKS):
+        to_sibling_near(j).wait_send()
+    lax.fori_loop(CHUNKS + WHOLE, CHUNKS + EXTRA, left_gather, 0)
     write(BLOCKS - 2).wait()
     write(BLOCKS - 1).wait()
 
@@ -412,21 +451,20 @@
         scratch_shapes=[
             pltpu.VMEM((CHUNKS + EXTRA, 2, 4, 2, 4, 16, LANES), BF16),
             pltpu.VMEM((2, D, COLS), BF16),
-            pltpu.VMEM((2 * SWAPPED, 2, ROWS, COLS), BF16),
+            pltpu.VMEM((NUMER + SENT, ROWS, COLS), BF16),
             pltpu.VMEM((2, 2, TOK // 2, COLS), F32),
             pltpu.VMEM((2, 2, TOK // 2, COLS), BF16),
             pltpu.VMEM((2, 2, TOK // 2, COLS), BF16),
             pltpu.VMEM((SENT, ROWS, COLS), BF16),
-            pltpu.VMEM((SENT, ROWS, COLS), BF16),
             pltpu.VMEM((4, 2, ROWS, COLS), BF16),
             pltpu.VMEM((BLOCKS, 2, ROWS, COLS), BF16),
-            dma((3,)),
+            dma((4,)),
             dma((5, CHUNKS + EXTRA, 4)),
             dma((5, CHUNKS + EXTRA, 4)),
             dma((WHOLE, GROUPS)),
             dma((WHOLE, GROUPS)),
-            dma((2 * SWAPPED,)),
-            dma((2 * SWAPPED,)),
+            dma((OVER,)),
+            dma((OVER,)),
             dma((GROUPS,)),
             dma((GROUPS,)),
             dma((SENT,)),

time: 152 us -> 146 us (0.961)
  Pallas kernels: 147 us -> 141 us
    pallas_call x1, Pallas kernels: 147 us -> 141 us  [shards(): pl.pallas_call(kernel, out_shape=jax.ShapeDtypeStruct((QUARTER, COLS), F3...]
where the time goes in v5:
time: 146 us
  Pallas kernels  141 us (97%)
  local copies, waits for them, and re-layouts  4.64 us (3%)
    pallas_call x1, Pallas kernels, shards(): pl.pallas_call(kernel, out_shape=jax.ShapeDtypeStruct((QUARTER, COLS), F3...  141 us
    unnamed x1, local copies, waits for them, and re-layouts  4.64 us

profile of v5, /device:TPU:1, one launch (start us, length us, event | category | flops | bytes accessed | tf_op | source)
XLA Modules:
  0.0 145.8 jit_solution(17248037812596512895)
XLA Ops:
  0.0 141.2 %merge.1 = f32[2048,512]{1,0:T(8,128)} custom-call(s32[2]{0:T(128)} %live.1, bf16[2,16,8192]{2,1,0:T(8,128)(2,1)} %tok.1, bf16[2,8192,512]{2,1,0:T(8,128)(2,1)} %wts.1, bf16[2,4,2,64,512]{4,3,2,1,0:T(8,128)(2,1)} %bitcast.1), custom_call_target="tpu_custom_call" | custom-call | flops 25769803776 | bytes 23068672 | tf_op jit(solution)/shard_map/merge/pallas_call | solution.py:446
  141.2 4.6 %copy.6 = f32[2048,512]{1,0:T(8,128)} copy(f32[2048,512]{1,0:T(8,128)} %merge.1) | data formatting | bytes 8388608

commit v6 on v5

--- a/solution.py
+++ b/solution.py
@@ -21,7 +21,7 @@
 QUARTER = D // 4
 BLOCKS = QUARTER // ROWS
 SWAPPED = 2
-PART = 128
+PART = 192
 OVER = 2 * (SWAPPED + 1)
 SENT = BLOCKS - SWAPPED
 ZERO = 2 * OVER
@@ -76,7 +76,7 @@
         )
 
     def seed(k):
-        part = xg.at[k, :, x, :, z]
+        part = xg.at[k, :, x, 0, z] if k is E0 else xg.at[k, :, x, :, z]
         return remote(part, part, g_send.at[0, k, 0], g_recv.at[0, k, 0], to_hi)
 
     def extra_seed(e, group, quarter):
@@ -93,7 +93,40 @@
         part = xg.at[CHUNKS + e, group % 2, :, 1 - group // 2]
         return remote(part, part, a_send.at[e, group], a_recv.at[e, group], to_alt)
 
+    def half_hops(step, k):
+        low, high = pl.ds(0, 512), pl.ds(512, 512)
+        if step == 1:
+            mine = [xg.at[k, q, x, 0, z] for q in range(2)]
+            return [
+                (mine[0], to_xr, xg.at[k, 0, xl, 0, z]),
+                (mine[0], to_xl, xg.at[k, 0, xr, 0, z]),
+                (mine[1], to_zr, xg.at[k, 1, x, 0, zl]),
+                (mine[1], to_zl, xg.at[k, 1, x, 0, zr]),
+            ]
+        if step == 2:
+            return [
+                (xg.at[k, 0, xl, 0, z, :, low], to_xr, xg.at[k, 0, x2, 0, z, :, low]),
+                (xg.at[k, 0, xr, 0, z, :, high], to_xl, xg.at[k, 0, x2, 0, z, :, high]),
+                (xg.at[k, 1, x, 0, zl, :, low], to_zr, xg.at[k, 1, x, 0, z2, :, low]),
+                (xg.at[k, 1, x, 0, zr, :, high], to_zl, xg.at[k, 1, x, 0, z2, :, high]),
+            ]
+        if step == 3:
+            return [
+                (xg.at[k, 0, :, 0, z], to_zr, xg.at[k, 0, :, 0, zl]),
+                (xg.at[k, 0, :, 0, z], to_zl, xg.at[k, 0, :, 0, zr]),
+                (xg.at[k, 1, x, 0], to_xr, xg.at[k, 1, xl, 0]),
+                (xg.at[k, 1, x, 0], to_xl, xg.at[k, 1, xr, 0]),
+            ]
+        return [
+            (xg.at[k, 0, :, 0, zl, :, low], to_zr, xg.at[k, 0, :, 0, z2, :, low]),
+            (xg.at[k, 0, :, 0, zr, :, high], to_zl, xg.at[k, 0, :, 0, z2, :, high]),
+            (xg.at[k, 1, xl, 0, :, :, low], to_xr, xg.at[k, 1, x2, 0, :, :, low]),
+            (xg.at[k, 1, xr, 0, :, :, high], to_xl, xg.at[k, 1, x2, 0, :, :, high]),
+        ]
+
     def hops(step, k):
+        if k is E0:
+            return half_hops(step, k)
         if step == 1:
             mine = [xg.at[k, q, x, :, z] for q in range(2)]
             return [
@@ -205,7 +238,7 @@
         @pl.when(i == 6)
         def _():
             for e in range(WHOLE, EXTRA):
-                for group in range(GROUPS):
+                for group in range(2 if e == WHOLE else 0, GROUPS):
                     for quarter in range(2):
                         extra_seed(e, group, quarter).start()
 
@@ -233,6 +266,11 @@
                 for e in range(WHOLE):
                     for quarter in range(2):
                         extra_whole(e, group, quarter).start()
+
+            @pl.when((k % 2 == 0) & (group < 2))
+            def _():
+                for quarter in range(2):
+                    extra_whole(WHOLE, group, quarter).start()
 
             for q in range(4):
                 rows = pl.ds(pl.multiple_of(half_base(k % 2) + q * LANES, LANES), LANES)
@@ -382,6 +420,8 @@
     for e in range(WHOLE):
         for group in range(GROUPS):
             extra_whole_all(e, group).wait_recv()
+    for group in range(2):
+        extra_whole_all(WHOLE, group).wait_recv()
     for n in range(OVER):
         weights_over(n).wait_recv()
 
@@ -397,8 +437,8 @@
         weights_over(n).wait_send()
     for g in range(GROUPS):
         resid_over(g).wait_send()
-    for e in range(WHOLE, EXTRA):
-        seed(CHUNKS + e).wait_send()
+    for k in (E0, E1, E2):
+        seed(k).wait_send()
 
     def near(j, carry):
         @pl.when(j >= 1)
@@ -430,20 +470,47 @@
     for e in range(WHOLE):
         for group in range(GROUPS):
             extra_whole_all(e, group).wait_send()
+    for group in range(2):
+        extra_whole_all(WHOLE, group).wait_send()
     to_partner_first().wait_send()
     for i in range(1, SENT):
         to_partner(i).wait_send()
     for j in range(BLOCKS - 4, BLOCKS):
         to_sibling_near(j).wait_send()
-    lax.fori_loop(CHUNKS + WHOLE, CHUNKS + EXTRA, left_gather, 0)
+    for k in (E0, E1, E2):
+        left_gather(k, 0)
     write(BLOCKS - 2).wait()
     write(BLOCKS - 1).wait()
+
+
+def place(src, dst, buf, ins, outs):
+    n = 8
+    rows = QUARTER // n
+    part = [pl.ds(i * rows, rows) for i in range(n)]
+    for i in range(n):
+        pltpu.make_async_copy(src.at[part[i]], buf.at[part[i]], ins.at[i]).start()
+    for i in range(n):
+        pltpu.make_async_copy(src.at[part[i]], buf.at[part[i]], ins.at[i]).wait()
+        pltpu.make_async_copy(buf.at[part[i]], dst.at[part[i]], outs.at[i]).start()
+    for i in range(n):
+        pltpu.make_async_copy(buf.at[part[i]], dst.at[part[i]], outs.at[i]).wait()
+
+
+def handed_on(merged):
+    return pl.pallas_call(
+        place,
+        out_shape=jax.ShapeDtypeStruct((QUARTER, COLS), F32),
+        in_specs=[pl.BlockSpec(memory_space=pl.ANY)],
+        out_specs=pl.BlockSpec(memory_space=pl.ANY),
+        scratch_shapes=[pltpu.VMEM((QUARTER, COLS), F32), pltpu.SemaphoreType.DMA((8,)), pltpu.SemaphoreType.DMA((8,))],
+        name="place",
+    )(merged)
 
 
 def shards(tokens, weights, targets, live):
     dma = pltpu.SemaphoreType.DMA
     any_space = pl.BlockSpec(memory_space=pl.ANY)
-    return pl.pallas_call(
+    return handed_on(pl.pallas_call(
         kernel,
         out_shape=jax.ShapeDtypeStruct((QUARTER, COLS), F32),
         in_specs=[pl.BlockSpec(memory_space=pltpu.SMEM), any_space, any_space, any_space],
@@ -461,8 +528,8 @@
             dma((4,)),
             dma((5, CHUNKS + EXTRA, 4)),
             dma((5, CHUNKS + EXTRA, 4)),
-            dma((WHOLE, GROUPS)),
-            dma((WHOLE, GROUPS)),
+            dma((WHOLE + 1, GROUPS)),
+            dma((WHOLE + 1, GROUPS)),
             dma((OVER,)),
             dma((OVER,)),
             dma((GROUPS,)),
@@ -482,7 +549,7 @@
             flops=3 * 2 * 2 * TOK * D * COLS, bytes_accessed=22 << 20, transcendentals=0
         ),
         name="merge",
-    )(live, tokens, weights, targets.reshape(2, 4, 2, 64, COLS))
+    )(live, tokens, weights, targets.reshape(2, 4, 2, 64, COLS)))
 
 
 def solution(mesh):

time: 146 us -> 143 us (0.979)
  local copies, waits for them, and re-layouts: 4.64 us -> 0 us
  Pallas kernels: 141 us -> 143 us
    unnamed x1 -> x0, local copies, waits for them, and re-layouts: 4.64 us -> none
    pallas_call x0 -> x1, Pallas kernels: none -> 3.58 us  [handed_on(): pl.pallas_call(place, out_shape=jax.ShapeDtypeStruct((QUARTER, COLS), F32...]
    pallas_call x1, Pallas kernels: 141 us -> 139 us  [shards(): pl.pallas_call(kernel, out_shape=jax.ShapeDtypeStruct((QUARTER, COLS), F3...]
where the time goes in v6:
time: 143 us
  Pallas kernels  143 us (100%)
    pallas_call x1, Pallas kernels, shards(): pl.pallas_call(kernel, out_shape=jax.ShapeDtypeStruct((QUARTER, COLS), F3...  139 us
    pallas_call x1, Pallas kernels, handed_on(): pl.pallas_call(place, out_shape=jax.ShapeDtypeStruct((QUARTER, COLS), F32...  3.58 us

profile of v6, /device:TPU:1, one launch (start us, length us, event | category | flops | bytes accessed | tf_op | source)
XLA Modules:
  0.0 142.7 jit_solution(3445608039862357829)
XLA Ops:
  0.0 139.1 %merge.1.src = f32[2048,512]{1,0:T(8,128)} custom-call(s32[2]{0:T(128)} %live.1, bf16[2,16,8192]{2,1,0:T(8,128)(2,1)} %tok.1, bf16[2,8192,512]{2,1,0:T(8,128)(2,1)} %wts.1, bf16[2,4,2,64,512]{4,3,2,1,0:T(8,128)(2,1)} %bitcast.1), custom_call_target="tpu_custom_call" | custom-call | flops 25769803776 | bytes 23068672 | tf_op jit(solution)/shard_map/merge/pallas_call | solution.py:513
  139.1 3.6 %place.1 = f32[2048,512]{1,0:T(8,128)} custom-call(f32[2048,512]{1,0:T(8,128)} %merge.1.src), custom_call_target="tpu_custom_call" | custom-call | tf_op jit(solution)/shard_map/place/pallas_call | solution.py:500

commit v7 on v6

--- a/solution.py
+++ b/solution.py
@@ -293,7 +293,7 @@
         inputs = jnp.concatenate(
             [first.reshape(TOK // 2, ROWS), second.reshape(TOK // 2, ROWS)], axis=0
         )
-        grad = SCALE * lax.dot_general(
+        grad = lax.dot_general(
             inputs, res.reshape(TOK, COLS), (((0,), (0,)), ((), ())), preferred_element_type=F32
         )
         return grad * grad
@@ -410,7 +410,7 @@
         def _():
             write(j - 2).wait()
 
-        acc[j % 2, 0] = numer / jnp.maximum(denom, 0.02)
+        acc[j % 2, 0] = numer / jnp.maximum(denom, 0.02 * D)
         write(j).start()
 
     follow(4, E0)

time: 143 us -> 143 us (level)
  no operation moved by 1% of the time
where the time goes in v7:
time: 143 us; the launch traced here: 142 us
  Pallas kernels  142 us (99%)
    pallas_call x1, Pallas kernels, shards(): pl.pallas_call(kernel, out_shape=jax.ShapeDtypeStruct((QUARTER, COLS), F3...  139 us
    pallas_call x1, Pallas kernels, handed_on(): pl.pallas_call(place, out_shape=jax.ShapeDtypeStruct((QUARTER, COLS), F32...  3.58 us

profile of v7, /device:TPU:1, one launch (start us, length us, event | category | flops | bytes accessed | tf_op | source)
XLA Modules:
  0.0 142.3 jit_solution(15563643033446622959)
XLA Ops:
  0.0 138.8 %merge.1.src = f32[2048,512]{1,0:T(8,128)} custom-call(s32[2]{0:T(128)} %live.1, bf16[2,16,8192]{2,1,0:T(8,128)(2,1)} %tok.1, bf16[2,8192,512]{2,1,0:T(8,128)(2,1)} %wts.1, bf16[2,4,2,64,512]{4,3,2,1,0:T(8,128)(2,1)} %bitcast.1), custom_call_target="tpu_custom_call" | custom-call | flops 25769803776 | bytes 23068672 | tf_op jit(solution)/shard_map/merge/pallas_call | solution.py:513
  138.8 3.6 %place.1 = f32[2048,512]{1,0:T(8,128)} custom-call(f32[2048,512]{1,0:T(8,128)} %merge.1.src), custom_call_target="tpu_custom_call" | custom-call | tf_op jit(solution)/shard_map/place/pallas_call | solution.py:500
